TPU v7x, 32 devices: a whole 2x2x4 slice. The times are simulated.
32 devices in a mesh: groups: 2 (over x), lat: 8 (over z, y), lev: 2 (over core).
Axes of the slice: x: 2, y: 2, z: 4, core: 2. Of those that a mesh axis runs over, the one named last changes fastest.
Arguments:
- state: float32 [256, 128, 1024], P(('groups', 'lat'), None, 'lev'), parts along dimension 0, may hold values from -6 to 6
- humidity: bfloat16 [256, 128, 1024], P(('groups', 'lat'), None, 'lev'), parts along dimension 0, may hold values from -6 to 6
- sun_list: int32 [16, 2, 64], P(('groups', 'lat'), 'lev'), parts along dimension 0, may hold values from 0 to 63, as said below
- sun_count: int32 [16, 2], P(('groups', 'lat'), 'lev'), parts along dimension 0, may hold values from 0 to 64, as said below
- w_in: bfloat16 [256, 256], replicated, may hold values from -0.375 to 0.375
- w_mid: bfloat16 [256, 256], replicated, may hold values from -0.375 to 0.375
- w_out: bfloat16 [256, 128], replicated, may hold values from -0.375 to 0.375
Outputs:
- new_state: float32 [256, 128, 1024], P(('groups', 'lat'), None, 'lev'), parts along dimension 0
There are 2 independent parts, one for each index of `groups`. A program takes and returns all parts, laid end to end along the dimension named above; an argument that names none is the same for every part. Nothing has to cross between parts.
Inputs may be any that keep to these rules, and one draw needn't show every extreme that they name: For every lat index i below 4 and lev index k, sun_count[i, k] + sun_count[i + 4, k] = 64, and sun_count[i, k] >= 32; the lat index 0 devices are fully sunlit. `sun_list`: each device's row is an ordering of its 64 blocks; its first sun_count entries are its sunlit blocks.
All inputs are finite; a program needn't handle non-finite values.
Results may differ from a plain program's by a relative error of at most 0.0024.
Values may be sent and summed in bfloat16 or wider, within the bound.
A program may use at most 128 MiB of HBM per device.

v0:
```python
import jax
import jax.numpy as jnp
from jax import lax
from jax.sharding import PartitionSpec as P

BLOCK = 128


damping_strength = 10.0


def legendre_table(order_values, nlat):
    colatitude = jnp.pi * (jnp.arange(nlat, dtype=jnp.float32) + 0.5) / nlat
    cosines = jnp.cos(colatitude)
    sines = jnp.sin(colatitude)
    weights = jnp.pi / nlat * sines
    order_float = order_values.astype(jnp.float32)[:, None]
    indices = jnp.arange(1, nlat, dtype=jnp.float32)
    log_steps = jnp.log((2.0 * indices + 1.0) / (2.0 * indices))
    cumulative = jnp.concatenate([jnp.zeros((1,), jnp.float32), jnp.cumsum(log_steps)])
    matches = jnp.arange(nlat, dtype=jnp.int32)[None, :] == order_values[:, None]
    picked = jnp.sum(jnp.where(matches, cumulative[None, :], 0.0), axis=1)
    diagonal = jnp.exp(
        0.5 * jnp.log(0.5) + 0.5 * picked[:, None] + order_float * jnp.log(sines)[None, :]
    )
    order_column = order_values[:, None]

    def recurrence(state_pair, degree):
        previous, earlier = state_pair
        degree_float = degree.astype(jnp.float32)
        first_step = jnp.sqrt(2.0 * order_float + 3.0) * cosines[None, :] * previous
        factor_now = jnp.sqrt(
            (4.0 * degree_float**2 - 1.0) / jnp.maximum(degree_float**2 - order_float**2, 1.0)
        )
        lower_degree = degree_float - 1.0
        factor_back = jnp.sqrt(
            jnp.maximum(lower_degree**2 - order_float**2, 0.0)
            / jnp.maximum(4.0 * lower_degree**2 - 1.0, 1.0)
        )
        general = factor_now * (cosines[None, :] * previous - factor_back * earlier)
        value = jnp.where(
            degree == order_column,
            diagonal,
            jnp.where(
                degree == order_column + 1,
                first_step,
                jnp.where(degree > order_column + 1, general, 0.0),
            ),
        )
        return ((value, previous), value)

    start = jnp.zeros((order_values.shape[0], nlat), jnp.float32)
    unused, values = lax.scan(
        recurrence, (start, start), jnp.arange(nlat, dtype=jnp.int32), unroll=64
    )
    return (jnp.transpose(values, (1, 2, 0)), weights)


def damping_factors(nlat):
    degrees = jnp.arange(nlat, dtype=jnp.float32)
    scaled = degrees * (degrees + 1.0) / ((nlat - 1.0) * nlat)
    return 1.0 / (1.0 + damping_strength * scaled**2) - 1.0


def radiation_net(blocks, w_in, w_mid, w_out):
    first = jnp.einsum("bfc,fh->bhc", blocks, w_in, preferred_element_type=jnp.float32)
    hidden_one = jax.nn.silu(first).astype(jnp.bfloat16)
    second = jnp.einsum("bhc,hk->bkc", hidden_one, w_mid, preferred_element_type=jnp.float32)
    hidden_two = jax.nn.silu(second).astype(jnp.bfloat16)
    output = jnp.einsum("bkc,kl->blc", hidden_two, w_out, preferred_element_type=jnp.float32)
    return output.astype(jnp.bfloat16)


def select_rows(row_ids, source):
    count = source.shape[0]
    picker = (row_ids[:, None] == jnp.arange(count, dtype=jnp.int32)[None, :]).astype(jnp.bfloat16)
    return jnp.einsum("sb,bfc->sfc", picker, source, preferred_element_type=jnp.float32).astype(
        jnp.bfloat16
    )


def local(state, humidity, sun_list, sun_count, w_in, w_mid, w_out):
    lat_dev, levels, half_lon = state.shape
    per_row = half_lon // BLOCK
    nblk = lat_dev * per_row
    lat_size = lax.axis_size("lat")
    lev_size = lax.axis_size("lev")
    nlat = lat_dev * lat_size
    nlon = half_lon * lev_size
    state_low = state.astype(jnp.bfloat16)

    def to_blocks(field):
        shaped = field.reshape(lat_dev, levels, per_row, BLOCK)
        return shaped.transpose(0, 2, 1, 3).reshape(nblk, levels, BLOCK)

    profiles = jnp.concatenate([to_blocks(state_low), to_blocks(humidity)], axis=1)
    listing = sun_list[0, 0]
    lit_count = sun_count[0, 0]
    positions = jnp.arange(nblk, dtype=jnp.int32)
    listed_heating = radiation_net(select_rows(listing, profiles), w_in, w_mid, w_out)
    placer = (listing[None, :] == positions[:, None]) & (positions[None, :] < lit_count)
    heating_blocks = jnp.einsum(
        "pb,blc->plc",
        placer.astype(jnp.bfloat16),
        listed_heating,
        preferred_element_type=jnp.float32,
    )
    heating_grid = heating_blocks.reshape(lat_dev, per_row, levels, BLOCK).transpose(0, 2, 1, 3)
    heating_grid = heating_grid.reshape(lat_dev, levels, half_lon)
    longitudes = lax.axis_index("lev") * half_lon + jnp.arange(half_lon, dtype=jnp.int32)
    wavenumbers = jnp.arange(nlat, dtype=jnp.int32)
    phase = longitudes[:, None] * wavenumbers[None, :] % nlon
    angle = phase.astype(jnp.float32) * (2.0 * jnp.pi / nlon)
    cos_table = jnp.cos(angle)
    sin_table = jnp.sin(angle)
    forward_tables = jnp.stack([cos_table, -sin_table]).astype(jnp.bfloat16)
    selected = forward_tables
    fourier = lax.psum_scatter(
        jnp.einsum("ilx,rxm->riml", state_low, selected, preferred_element_type=jnp.float32) / nlon,
        "lev",
        scatter_dimension=0,
        tiled=True,
    ).astype(jnp.bfloat16)
    by_wave = lax.all_to_all(fourier, "lat", split_axis=2, concat_axis=1, tiled=True)
    owned = lax.axis_index("lat") * lat_dev + jnp.arange(lat_dev, dtype=jnp.int32)
    table, weights = legendre_table(owned, nlat)
    analysis = (table * weights[None, :, None]).astype(jnp.bfloat16)
    synthesis = table.astype(jnp.bfloat16)
    spectral = jnp.einsum("rjml,mjn->rmnl", by_wave, analysis, preferred_element_type=jnp.float32)
    damped = (spectral * damping_factors(nlat)[None, None, :, None]).astype(jnp.bfloat16)
    back_four = jnp.einsum(
        "rmnl,mjn->rjml", damped, synthesis, preferred_element_type=jnp.float32
    ).astype(jnp.bfloat16)
    by_lat = lax.all_to_all(back_four, "lat", split_axis=1, concat_axis=2, tiled=True)
    multiplicity = jnp.where(wavenumbers == 0, 1.0, 2.0).astype(jnp.float32)
    inverse_tables = jnp.stack(
        [cos_table.T * multiplicity[:, None], -sin_table.T * multiplicity[:, None]]
    ).astype(jnp.bfloat16)
    selected = inverse_tables
    increment = jnp.einsum(
        "riml,rmx->ilx",
        lax.all_gather(by_lat, "lev", axis=0, tiled=True),
        selected,
        preferred_element_type=jnp.float32,
    )
    return state + heating_grid + increment


def solution(mesh):
    return jax.shard_map(
        local,
        mesh=mesh,
        in_specs=(
            P(("groups", "lat"), None, "lev"),
            P(("groups", "lat"), None, "lev"),
            P(("groups", "lat"), "lev", None),
            P(("groups", "lat"), "lev"),
            P(),
            P(),
            P(),
        ),
        out_specs=P(("groups", "lat"), None, "lev"),
        check_vma=False,
    )
```

profile of v0, /device:TPU:1, one launch (start us, length us, event | category | flops | bytes accessed | tf_op | source)
XLA Modules:
  0.0 517.5 jit_solution(6932854627741029909)
XLA Ops:
  7.7 2.5 convert_element_type.543
  10.2 2.1 multiply_bitcast_fusion
  13.5 416.7 %while.21 = (s32[]{:T(128)}, f32[16,128]{1,0:T(8,128)S(1)}, f32[16,128]{1,0:T(8,128)S(1)}, f32[2,64,16,128]{3,2,1,0:T(8,128)S(1)}, s32[2,64]{1,0:T(2,128)}, /*in...) while((s32[]{:T(128)}, f32[16,128]{1,0:T(8,128)S(1)}, ...), condition=%wide.region_3.4_spmd.clone.clone.clone.clone, body=%wide.region_2.3_spmd.clone.clone.clone.clone.sunk | while | flops 1464210 | bytes 3412516 | solution.py:53
  69.6 1.9 compare_bitcast_fusion.357
  73.9 1.9 compare_bitcast_fusion.360
  118.7 1.9 compare_bitcast_fusion.321
  123.0 1.9 compare_bitcast_fusion.324
  131.6 1.9 compare_bitcast_fusion.330
  277.9 1.9 compare_bitcast_fusion.357
  282.3 1.9 compare_bitcast_fusion.360
  327.1 1.9 compare_bitcast_fusion.321
  331.3 1.9 compare_bitcast_fusion.324
  335.7 1.9 compare_bitcast_fusion.327
  432.1 2.7 copy.39
  437.2 6.4 %all-to-all-start = ((bf16[1,16,128,128]{3,1,0,2:T(8,128)(2,1)}), bf16[1,16,128,128]{3,1,0,2:T(8,128)(2,1)}, u32[]{:S(2)}, u32[]{:S(2)}) async-start(bf16[1,16,128,128]{3,1,0,2:T(8,128)(2,1)} %copy.46), calls=%async_computation.1 | async-start | bytes 1048576 | tf_op jit(solution)/shard_map/all_to_all | solution.py:124
  447.1 4.3 fusion.163
  451.4 5.8 %all-to-all-done = bf16[1,16,128,128]{3,1,0,2:T(8,128)(2,1)} async-done(((bf16[1,16,128,128]{3,1,0,2:T(8,128)(2,1)}), bf16[1,16,128,128]{3,1,0,2:T(8,128)(2,1)}, u32[]{:S(2)}, u32[]{:S(2)}) %all-to-all-start) | async-done | bytes 524320 | tf_op jit(solution)/shard_map/all_to_all | solution.py:124
  461.2 4.9 all-to-all-start.1
  466.2 14.4 %fusion.159 = f32[64,128,256]{2,1,0:T(8,128)} fusion(bf16[64,256,128]{2,0,1:T(8,128)(2,1)} %fusion.163, bf16[256,256]{1,0:T(8,128)(2,1)S(1)} %copy-done, bf16[256,256]{1,0:T(8,128)(2,1)S(1)} %copy-done.5), kind=kOutput, calls=%fused_computation.616 | convolution fusion | flops 2157969408 | bytes 12845056 | tf_op jit(solution)/shard_map/bhc,hk->bkc/dot_general | solution.py:68
  481.7 7.0 %convert_bitcast_fusion = bf16[64,128,128]{1,2,0:T(8,128)(2,1)} fusion(f32[64,128,256]{2,1,0:T(8,128)} %fusion.159, bf16[256,128]{1,0:T(8,128)(2,1)S(1)} %copy-done.6), kind=kOutput, calls=%fused_computation.624 | convolution fusion | flops 548405248 | bytes 10551296 | tf_op jit(solution)/shard_map/bkc,kl->blc/dot_general | solution.py:70
  489.4 3.6 copy.42
  493.0 2.7 fusion.212
  495.7 5.5 %reshape.4467 = f32[16,128,512]{2,0,1:T(8,128)} reshape(f32[16,128,4,128]{3,2,0,1:T(4,128)} %bitcast.1514) | data formatting | bytes 8388608 | tf_op jit(solution)/shard_map/reshape | solution.py:109
  502.3 8.4 %bitcast_add_fusion = f32[16,128,512]{2,1,0:T(8,128)} fusion(f32[16,128,512]{2,1,0:T(8,128)} %param.9, f32[16,128,512]{2,0,1:T(8,128)} %reshape.4467, bf16[2,16,128,128]{2,3,0,1:T(8,128)(2,1)} %all-gather.2.cloned.1.call-done, bf16[1,128,512]{2,1,0:T(8,128)(2,1)S(1)} %get-tuple-element.1389, bf16[1,128,512]{2,1,0:T(8,128)(2,1)S(1)} %get-tuple-element.1388), kind=kOutput, calls=%fused_computation.612 | convolution fusion | flops 539099136 | bytes 13893632 | tf_op jit(solution)/shard_map/riml,rmx->ilx/dot_general | solution.py:140
  (507 shorter events, 331.7 us)
Async XLA Ops:
  6.5 459.6 %copy-start = (bf16[256,256]{1,0:T(8,128)(2,1)S(1)}, bf16[256,256]{1,0:T(8,128)(2,1)}, u32[]{:S(2)}) copy-start(bf16[256,256]{1,0:T(8,128)(2,1)} %param.14) | copy-start | bytes 393220
  6.5 428.2 %reduce-scatter.2.cloned.1.call-start = ((), (), s32[]{:S(2)}) async-start(), calls=%async_computation.3 | async-start | bytes 3145728 | tf_op jit(solution)/shard_map/reduce_scatter | solution.py:118
  6.5 5.7 %copy-start.2 = (s32[512]{0:T(512)}, s32[512]{0:T(512)S(1)}, u32[]{:S(2)}) copy-start(s32[512]{0:T(512)S(1)} %iota_add_fusion.1) | copy-start | bytes 6148
  437.2 19.9 %all-to-all-start = ((bf16[1,16,128,128]{3,1,0,2:T(8,128)(2,1)}), bf16[1,16,128,128]{3,1,0,2:T(8,128)(2,1)}, u32[]{:S(2)}, u32[]{:S(2)}) async-start(bf16[1,16,128,128]{3,1,0,2:T(8,128)(2,1)} %copy.46), calls=%async_computation.1 | async-start | bytes 1048576 | tf_op jit(solution)/shard_map/all_to_all | solution.py:124
  445.4 1.6 copy-start.1
  445.5 1.6 copy-start.4
  451.4 14.8 %copy-start.5 = (bf16[256,256]{1,0:T(8,128)(2,1)S(1)}, bf16[256,256]{1,0:T(8,128)(2,1)}, u32[]{:S(2)}) copy-start(bf16[256,256]{1,0:T(8,128)(2,1)} %param.13) | copy-start | bytes 393220
  461.2 19.4 %all-to-all-start.1 = ((bf16[1,128,16,128]{3,2,0,1:T(8,128)(2,1)}), bf16[1,128,16,128]{3,2,0,1:T(8,128)(2,1)S(1)}, u32[]{:S(2)}, u32[]{:S(2)}) async-start(bf16[1,128,16,128]{3,2,0,1:T(8,128)(2,1)} %copy.50), calls=%async_computation.2 | async-start | bytes 1048576 | tf_op jit(solution)/shard_map/all_to_all | solution.py:134
  466.1 15.6 %copy-start.6 = (bf16[256,128]{1,0:T(8,128)(2,1)S(1)}, bf16[256,128]{1,0:T(8,128)(2,1)}, u32[]{:S(2)}) copy-start(bf16[256,128]{1,0:T(8,128)(2,1)} %param.15) | copy-start | bytes 196612
  466.1 36.2 %all-gather.2.cloned.1.call-start = ((), (), s32[]{:S(2)}) async-start(), calls=%async_computation.4 | async-start | bytes 1572864 | tf_op jit(solution)/shard_map/all_gather | solution.py:142
  495.7 5.5 %copy-start.3 = (s32[512]{0:T(512)S(1)}, s32[512]{0:T(512)}, u32[]{:S(2)}) copy-start(s32[512]{0:T(512)} %copy-done.2) | copy-start | bytes 6148
Sparse Core Ops, SparseCore 0:
  12.4 12.0 reduce-scatter.1
  481.8 10.8 all-gather.1
where the time goes:
time: 523 us; the launch traced here: 518 us
  other arithmetic  335 us (64%)
  loops' own time  82.4 us (16%)
  matrix products  40.6 us (8%)
  local copies, waits for them, and re-layouts  28.4 us (5%)
  between operations  14.3 us (3%)
  starting transfers between devices  11.3 us (2%)
  waiting for transfers between devices  5.84 us (1%)
    eq x128, other arithmetic, recurrence(): degree == order_column + 1  131 us
    gt x64, other arithmetic, recurrence(): degree > order_column + 1  100 us
    another operation x1, loops' own time, legendre_table(): lax.scan(recurrence, (start, start), jnp.arange(nlat, dtype=jnp.int32), u...  82.4 us
    while x126, other arithmetic  71.4 us
    sqrt x128, other arithmetic, recurrence(): jnp.sqrt((4.0 * degree_float ** 2 - 1.0) / jnp.maximum(degree_float ** 2...  24 us
    dot_general x1, matrix products, radiation_net(): jnp.einsum('bhc,hk->bkc', hidden_one, w_mid, preferred_element_type=jnp.f...  14.4 us
  transfers between devices with their start and end apart: 4, of which 1 were waited for; matrix products, arithmetic and copies ran while one was open for 74% of the time, Pallas kernels for 0%

commit v1 on v0

--- a/solution.py
+++ b/solution.py
@@ -1,6 +1,8 @@
 import jax
 import jax.numpy as jnp
 from jax import lax
+from jax.experimental import pallas as pl
+from jax.experimental.pallas import tpu as pltpu
 from jax.sharding import PartitionSpec as P
 
 BLOCK = 128
@@ -9,7 +11,38 @@
 damping_strength = 10.0
 
 
-def legendre_table(order_values, nlat):
+def legendre_rows(order, cosines, diagonal_ref, out_ref, nlat):
+    order_float = order.astype(jnp.float32)
+    order_square = order_float * order_float
+
+    def step(degree, pair):
+        previous, earlier = pair
+        degree_float = degree.astype(jnp.float32)
+        square = degree_float * degree_float
+        lower = degree_float - 1.0
+        lower_square = lower * lower
+        factor_now = jnp.sqrt((4.0 * square - 1.0) / jnp.maximum(square - order_square, 1.0))
+        factor_back = jnp.sqrt(
+            jnp.maximum(lower_square - order_square, 0.0)
+            / jnp.maximum(4.0 * lower_square - 1.0, 1.0)
+        )
+        general = factor_now * (cosines * previous - factor_back * earlier)
+        value = jnp.where(degree == order, diagonal_ref[...], jnp.where(degree > order, general, 0.0))
+        out_ref[degree] = value
+        return value, previous
+
+    start = diagonal_ref[...] * 0.0
+    lax.fori_loop(0, nlat, step, (start, start), unroll=8)
+
+
+def legendre_kernel(cosine_ref, diagonal_ref, out_ref):
+    nlat = out_ref.shape[0]
+    orders = diagonal_ref.shape[0]
+    order = lax.axis_index("lat") * orders + lax.broadcasted_iota(jnp.int32, diagonal_ref.shape, 0)
+    legendre_rows(order, cosine_ref[...], diagonal_ref, out_ref, nlat)
+
+
+def legendre_inputs(order_values, nlat):
     colatitude = jnp.pi * (jnp.arange(nlat, dtype=jnp.float32) + 0.5) / nlat
     cosines = jnp.cos(colatitude)
     sines = jnp.sin(colatitude)
@@ -17,43 +50,22 @@
     order_float = order_values.astype(jnp.float32)[:, None]
     indices = jnp.arange(1, nlat, dtype=jnp.float32)
     log_steps = jnp.log((2.0 * indices + 1.0) / (2.0 * indices))
-    cumulative = jnp.concatenate([jnp.zeros((1,), jnp.float32), jnp.cumsum(log_steps)])
-    matches = jnp.arange(nlat, dtype=jnp.int32)[None, :] == order_values[:, None]
-    picked = jnp.sum(jnp.where(matches, cumulative[None, :], 0.0), axis=1)
+    below = jnp.arange(1, nlat, dtype=jnp.int32)[None, :] <= order_values[:, None]
+    picked = jnp.sum(jnp.where(below, log_steps[None, :], 0.0), axis=1)
     diagonal = jnp.exp(
         0.5 * jnp.log(0.5) + 0.5 * picked[:, None] + order_float * jnp.log(sines)[None, :]
     )
-    order_column = order_values[:, None]
+    return cosines, weights, diagonal
 
-    def recurrence(state_pair, degree):
-        previous, earlier = state_pair
-        degree_float = degree.astype(jnp.float32)
-        first_step = jnp.sqrt(2.0 * order_float + 3.0) * cosines[None, :] * previous
-        factor_now = jnp.sqrt(
-            (4.0 * degree_float**2 - 1.0) / jnp.maximum(degree_float**2 - order_float**2, 1.0)
-        )
-        lower_degree = degree_float - 1.0
-        factor_back = jnp.sqrt(
-            jnp.maximum(lower_degree**2 - order_float**2, 0.0)
-            / jnp.maximum(4.0 * lower_degree**2 - 1.0, 1.0)
-        )
-        general = factor_now * (cosines[None, :] * previous - factor_back * earlier)
-        value = jnp.where(
-            degree == order_column,
-            diagonal,
-            jnp.where(
-                degree == order_column + 1,
-                first_step,
-                jnp.where(degree > order_column + 1, general, 0.0),
-            ),
-        )
-        return ((value, previous), value)
 
-    start = jnp.zeros((order_values.shape[0], nlat), jnp.float32)
-    unused, values = lax.scan(
-        recurrence, (start, start), jnp.arange(nlat, dtype=jnp.int32), unroll=64
-    )
-    return (jnp.transpose(values, (1, 2, 0)), weights)
+def legendre_table(order_values, nlat):
+    cosines, weights, diagonal = legendre_inputs(order_values, nlat)
+    table = pl.pallas_call(
+        legendre_kernel,
+        out_shape=jax.ShapeDtypeStruct((nlat,) + diagonal.shape, jnp.float32),
+        compiler_params=pltpu.CompilerParams(vmem_limit_bytes=48 * 2**20),
+    )(jnp.broadcast_to(cosines[None, :], diagonal.shape), diagonal)
+    return table, weights
 
 
 def damping_factors(nlat):
@@ -124,12 +136,12 @@
     by_wave = lax.all_to_all(fourier, "lat", split_axis=2, concat_axis=1, tiled=True)
     owned = lax.axis_index("lat") * lat_dev + jnp.arange(lat_dev, dtype=jnp.int32)
     table, weights = legendre_table(owned, nlat)
-    analysis = (table * weights[None, :, None]).astype(jnp.bfloat16)
+    analysis = (table * weights[None, None, :]).astype(jnp.bfloat16)
     synthesis = table.astype(jnp.bfloat16)
-    spectral = jnp.einsum("rjml,mjn->rmnl", by_wave, analysis, preferred_element_type=jnp.float32)
+    spectral = jnp.einsum("rjml,nmj->rmnl", by_wave, analysis, preferred_element_type=jnp.float32)
     damped = (spectral * damping_factors(nlat)[None, None, :, None]).astype(jnp.bfloat16)
     back_four = jnp.einsum(
-        "rmnl,mjn->rjml", damped, synthesis, preferred_element_type=jnp.float32
+        "rmnl,nmj->rjml", damped, synthesis, preferred_element_type=jnp.float32
     ).astype(jnp.bfloat16)
     by_lat = lax.all_to_all(back_four, "lat", split_axis=1, concat_axis=2, tiled=True)
     multiplicity = jnp.where(wavenumbers == 0, 1.0, 2.0).astype(jnp.float32)

time: 523 us -> 107 us (0.20)
  other arithmetic: 335 us -> 7.77 us
  loops' own time: 82.4 us -> 0 us
  local copies, waits for them, and re-layouts: 28.4 us -> 17.9 us
  waiting for transfers between devices: 5.84 us -> 13.4 us
    eq x128 -> x0, other arithmetic: 131 us -> none  [recurrence(): degree == order_column + 1]
    gt x64 -> x0, other arithmetic: 100 us -> none  [recurrence(): degree > order_column + 1]
    another operation x1 -> x0, loops' own time: 82.4 us -> none  [legendre_table(): lax.scan(recurrence, (start, start), jnp.arange(nlat, dtype=jnp.int32), u...]
    while x126 -> x0, other arithmetic: 71.4 us -> none
    sqrt x130 -> x0, other arithmetic: 24 us -> none  [the longest x128 24 us: recurrence(): jnp.sqrt((4.0 * degree_float ** 2 - 1.0) / jnp.maximum(degree_float ** 2...]
    reduce_scatter x1, waiting for transfers between devices: 0.01 us -> 6.21 us  [local(): lax.psum_scatter(jnp.einsum('ilx,rxm->riml', state_low, selected, preferr...]
  transfers between devices with their start and end apart: 4 -> 4, of which waited for: 1 -> 2; matrix products, arithmetic and copies ran while one was open for 74% -> 43% of each run, Pallas kernels for 0% -> 1%
where the time goes in v1:
time: 107 us; the launch traced here: 105 us
  matrix products  40.4 us (38%)
  local copies, waits for them, and re-layouts  17.9 us (17%)
  between operations  14.3 us (13%)
  waiting for transfers between devices  13.4 us (13%)
  starting transfers between devices  10.3 us (10%)
  other arithmetic  7.77 us (7%)
  Pallas kernels  1.3 us (1%)
    dot_general x1, matrix products, radiation_net(): jnp.einsum('bhc,hk->bkc', hidden_one, w_mid, preferred_element_type=jnp.f...  14.4 us
    dot_general x1, matrix products, local(): jnp.einsum('riml,rmx->ilx', lax.all_gather(by_lat, 'lev', axis=0, tiled=T...  8.38 us
    all_to_all x1, waiting for transfers between devices, local(): lax.all_to_all(fourier, 'lat', split_axis=2, concat_axis=1, tiled=True)  7.17 us
    dot_general x1, matrix products, radiation_net(): jnp.einsum('bkc,kl->blc', hidden_two, w_out, preferred_element_type=jnp.f...  7.02 us
    reduce_scatter x1, waiting for transfers between devices, local(): lax.psum_scatter(jnp.einsum('ilx,rxm->riml', state_low, selected, preferr...  6.21 us
    all_to_all x1, starting transfers between devices, local(): lax.all_to_all(fourier, 'lat', split_axis=2, concat_axis=1, tiled=True)  5.6 us
    reshape x1, local copies, waits for them, and re-layouts, local(): heating_grid = heating_grid.reshape(lat_dev, levels, half_lon)  5.49 us
    all_to_all x1, starting transfers between devices, local(): lax.all_to_all(back_four, 'lat', split_axis=1, concat_axis=2, tiled=True)  4.52 us
  transfers between devices with their start and end apart: 4, of which 2 were waited for; matrix products, arithmetic and copies ran while one was open for 43% of the time, Pallas kernels for 1%

profile of v1, /device:TPU:1, one launch (start us, length us, event | category | flops | bytes accessed | tf_op | source)
XLA Modules:
  0.0 105.3 jit_solution(6315656554693316462)
XLA Ops:
  6.5 1.1 %cosine_convert_fusion = (bf16[1,512,128]{1,2,0:T(8,128)(2,1)S(1)}, bf16[1,512,128]{1,2,0:T(8,128)(2,1)S(1)}) fusion(s32[512]{0:T(512)S(1)} %iota_add_fusion), kind=kLoop, calls=%fused_computation.61 | loop fusion | flops 1114112 | bytes 264192 | tf_op jit(solution)/shard_map/convert.2
  7.6 2.5 %convert_element_type.80 = bf16[16,128,512]{2,1,0:T(8,128)(2,1)S(1)} convert(f32[16,128,512]{2,1,0:T(8,128)} %param.7) | non-fusion elementwise | flops 1048576 | bytes 6291456 | tf_op jit(solution)/shard_map/convert_element_type | solution.py:102
  10.1 2.1 %multiply_bitcast_fusion = f32[2,16,128,128]{3,2,1,0:T(8,128)} fusion(bf16[16,128,512]{2,1,0:T(8,128)(2,1)S(1)} %convert_element_type.80, bf16[1,512,128]{1,2,0:T(8,128)(2,1)S(1)} %get-tuple-element.18, bf16[1,512,128]{1,2,0:T(8,128)(2,1)S(1)} %get-tuple-element.17), kind=kOutput, calls=%fused_computation.27 | convolution fusion | flops 537919488 | bytes 4456448 | tf_op jit(solution)/shard_map/ilx,rxm->riml/dot_general | solution.py:131
  13.0 1.4 %copy.39 = bf16[64,128,128]{2,0,1:T(8,128)(2,1)S(1)} copy(bf16[64,128,128]{2,1,0:T(8,128)(2,1)S(1)} %bitcast.91) | data formatting | bytes 4194304 | tf_op jit(solution)/shard_map/reshape | solution.py:106
  15.2 2.7 %copy.40 = bf16[64,128,128]{2,0,1:T(8,128)(2,1)} copy(bf16[64,128,128]{2,1,0:T(8,128)(2,1)S(1)} %bitcast.92) | data formatting | bytes 4194304 | tf_op jit(solution)/shard_map/reshape | solution.py:106
  18.2 6.2 %reduce-scatter.2.cloned.1.call-done = f32[1,16,128,128]{3,2,1,0:T(8,128)} async-done(((f32[2,16,128,128]{3,2,1,0:T(8,128)}), f32[1,16,128,128]{3,2,1,0:T(8,128)}) %reduce-scatter.2.cloned.1.call-update) | async-done | bytes 1048592 | tf_op jit(solution)/shard_map/reduce_scatter | solution.py:130
  24.4 1.3 %convert_element_type.90 = bf16[1,16,128,128]{3,2,1,0:T(8,128)(2,1)S(1)} convert(f32[1,16,128,128]{3,2,1,0:T(8,128)} %reduce-scatter.2.cloned.1.call-done) | non-fusion elementwise | flops 262144 | bytes 1572864 | tf_op jit(solution)/shard_map/convert_element_type | solution.py:135
  25.8 1.1 %copy.44 = bf16[1,16,128,128]{3,1,0,2:T(8,128)(2,1)} copy(bf16[1,16,128,128]{3,2,1,0:T(8,128)(2,1)S(1)} %convert_element_type.90) | data formatting | bytes 1048576 | tf_op jit(solution)/shard_map/convert_element_type | solution.py:135
  26.9 5.6 %all-to-all-start = ((bf16[1,16,128,128]{3,1,0,2:T(8,128)(2,1)}), bf16[1,16,128,128]{3,1,0,2:T(8,128)(2,1)S(1)}, u32[]{:S(2)}, u32[]{:S(2)}) async-start(bf16[1,16,128,128]{3,1,0,2:T(8,128)(2,1)} %copy.44), calls=%async_computation.1 | async-start | bytes 1048576 | tf_op jit(solution)/shard_map/all_to_all | solution.py:136
  32.6 1.3 %shard_map.73 = f32[128,16,128]{2,1,0:T(8,128)S(1)} custom-call(f32[16,128]{1,0:T(8,128)S(1)} %broadcast_in_dim.18.cosine_ref, f32[16,128]{1,0:T(8,128)S(1)} %add_exponential_fusion.diagonal_ref), custom_call_target="tpu_custom_call" | custom-call | tf_op jit(solution)/shard_map/pallas_call | solution.py:63
  33.9 0.9 multiply_convert_fusion
  34.9 4.2 %fusion.18 = bf16[64,256,128]{2,0,1:T(8,128)(2,1)} fusion(bf16[64,128,128]{2,0,1:T(8,128)(2,1)S(1)} %copy-done.1, bf16[64,128,128]{2,0,1:T(8,128)(2,1)S(1)} %copy.39, s32[64]{0:T(128)S(1)} %bitcast.97), kind=kOutput, calls=%fused_computation.22 | convolution fusion | flops 278925312 | bytes 8388864 | tf_op jit(solution)/shard_map/sb,bfc->sfc/dot_general | solution.py:89
  39.1 7.2 %all-to-all-done = bf16[1,16,128,128]{3,1,0,2:T(8,128)(2,1)S(1)} async-done(((bf16[1,16,128,128]{3,1,0,2:T(8,128)(2,1)}), bf16[1,16,128,128]{3,1,0,2:T(8,128)(2,1)S(1)}, u32[]{:S(2)}, u32[]{:S(2)}) %all-to-all-start) | async-done | bytes 524320 | tf_op jit(solution)/shard_map/all_to_all | solution.py:136
  46.5 1.5 %fusion.32 = bf16[1,128,16,128]{3,1,2,0:T(8,128)(2,1)S(1)} fusion(bf16[128,16,128]{2,1,0:T(8,128)(2,1)} %get-tuple-element.14, bf16[128,16,128]{2,1,0:T(8,128)(2,1)S(1)} %bitcast.96, bf16[128,16,128]{2,1,0:T(8,128)(2,1)S(1)} %get-tuple-element.13, f32[128]{0:T(128)S(1)} %fusion.74), kind=kOutput, calls=%fused_computation.32 | convolution fusion | flops 135004160 | bytes 2097664 | tf_op jit(solution)/shard_map/rmnl,nmj->rjml/dot_general | solution.py:143
  48.0 1.2 %copy.50 = bf16[1,128,16,128]{3,2,0,1:T(8,128)(2,1)} copy(bf16[1,128,16,128]{3,1,2,0:T(8,128)(2,1)S(1)} %fusion.32) | data formatting | bytes 1048576 | tf_op jit(solution)/shard_map/convert_element_type | solution.py:145
  49.2 4.5 %all-to-all-start.1 = ((bf16[1,128,16,128]{3,2,0,1:T(8,128)(2,1)}), bf16[1,128,16,128]{3,2,0,1:T(8,128)(2,1)S(1)}, u32[]{:S(2)}, u32[]{:S(2)}) async-start(bf16[1,128,16,128]{3,2,0,1:T(8,128)(2,1)} %copy.50), calls=%async_computation.2 | async-start | bytes 1048576 | tf_op jit(solution)/shard_map/all_to_all | solution.py:146
  54.0 14.4 %fusion.14 = f32[64,128,256]{2,1,0:T(8,128)} fusion(bf16[64,256,128]{2,0,1:T(8,128)(2,1)} %fusion.18, bf16[256,256]{1,0:T(8,128)(2,1)S(1)} %copy-done, bf16[256,256]{1,0:T(8,128)(2,1)S(1)} %copy-done.4), kind=kOutput, calls=%fused_computation.20 | convolution fusion | flops 2157969408 | bytes 12845056 | tf_op jit(solution)/shard_map/bhc,hk->bkc/dot_general | solution.py:80
  68.4 1.0 copy.52
  69.5 7.0 %convert_bitcast_fusion = bf16[64,128,128]{1,2,0:T(8,128)(2,1)} fusion(f32[64,128,256]{2,1,0:T(8,128)} %fusion.14, bf16[256,128]{1,0:T(8,128)(2,1)S(1)} %copy-done.5), kind=kOutput, calls=%fused_computation.28 | convolution fusion | flops 548405248 | bytes 10551296 | tf_op jit(solution)/shard_map/bkc,kl->blc/dot_general | solution.py:82
  77.2 3.6 %copy.42 = bf16[64,128,128]{2,0,1:T(8,128)(2,1)S(1)} copy(bf16[64,128,128]{1,2,0:T(8,128)(2,1)} %convert_bitcast_fusion) | data formatting | bytes 4194304 | tf_op jit(solution)/shard_map/convert_element_type | solution.py:83
  80.8 2.7 %fusion.61 = f32[64,128,128]{2,0,1:T(8,128)} fusion(bf16[64,128,128]{2,0,1:T(8,128)(2,1)S(1)} %copy.42, s32[64]{0:T(128)S(1)} %bitcast.98, pred[64]{0:T(512)(128)(4,1)S(1)} %iota_compare_fusion.2), kind=kOutput, calls=%fused_computation.73 | convolution fusion | flops 134225920 | bytes 6291776 | tf_op jit(solution)/shard_map/pb,blc->plc/dot_general | solution.py:114
  83.5 5.5 %reshape.358 = f32[16,128,512]{2,0,1:T(8,128)} reshape(f32[16,128,4,128]{3,2,0,1:T(4,128)} %bitcast.90) | data formatting | bytes 8388608 | tf_op jit(solution)/shard_map/reshape | solution.py:121
  89.0 1.1 %multiply_convert_fusion.2 = (bf16[1,128,512]{2,1,0:T(8,128)(2,1)S(1)}, bf16[1,128,512]{2,1,0:T(8,128)(2,1)S(1)}) fusion(f32[128]{0:T(128)S(1)} %compare_select_fusion, s32[512]{0:T(512)S(1)} %iota_add_fusion), kind=kLoop, calls=%fused_computation.57 | loop fusion | flops 1245184 | bytes 264704 | tf_op jit(solution)/shard_map/convert
  90.1 8.4 %bitcast_add_fusion = f32[16,128,512]{2,1,0:T(8,128)} fusion(f32[16,128,512]{2,1,0:T(8,128)} %param.7, f32[16,128,512]{2,0,1:T(8,128)} %reshape.358, bf16[2,16,128,128]{2,3,0,1:T(8,128)(2,1)} %all-gather.2.cloned.1.call-done, bf16[1,128,512]{2,1,0:T(8,128)(2,1)S(1)} %get-tuple-element.16, bf16[1,128,512]{2,1,0:T(8,128)(2,1)S(1)} %get-tuple-element.15), kind=kOutput, calls=%fused_computation.16 | convolution fusion | flops 539099136 | bytes 13893632 | tf_op jit(solution)/shard_map/riml,rmx->ilx/dot_general | solution.py:152
  (39 shorter events, 2.5 us)
Async XLA Ops:
  6.5 47.4 %copy-start = (bf16[256,256]{1,0:T(8,128)(2,1)S(1)}, bf16[256,256]{1,0:T(8,128)(2,1)}, u32[]{:S(2)}) copy-start(bf16[256,256]{1,0:T(8,128)(2,1)} %param.12) | copy-start | bytes 393220
  6.5 17.9 %reduce-scatter.2.cloned.1.call-start = ((), (), s32[]{:S(2)}) async-start(), calls=%async_computation.3 | async-start | bytes 3145728 | tf_op jit(solution)/shard_map/reduce_scatter | solution.py:130
  12.8 1.6 %copy-start.2 = (bf16[16,128,512]{2,1,0:T(8,128)(2,1)S(1)}, bf16[16,128,512]{2,1,0:T(8,128)(2,1)}, u32[]{:S(2)}) copy-start(bf16[16,128,512]{2,1,0:T(8,128)(2,1)} %param.8) | copy-start | bytes 6291460
  17.9 17.0 %copy-start.3 = (s32[1,1,64]{2,1,0:T(1,128)S(1)}, s32[1,1,64]{2,1,0:T(1,128)}, u32[]{:S(2)}) copy-start(s32[1,1,64]{2,1,0:T(1,128)} %param.9) | copy-start | bytes 772
  26.9 19.4 %all-to-all-start = ((bf16[1,16,128,128]{3,1,0,2:T(8,128)(2,1)}), bf16[1,16,128,128]{3,1,0,2:T(8,128)(2,1)S(1)}, u32[]{:S(2)}, u32[]{:S(2)}) async-start(bf16[1,16,128,128]{3,1,0,2:T(8,128)(2,1)} %copy.44), calls=%async_computation.1 | async-start | bytes 1048576 | tf_op jit(solution)/shard_map/all_to_all | solution.py:136
  32.5 2.4 %copy-start.1 = (bf16[64,128,128]{2,0,1:T(8,128)(2,1)S(1)}, bf16[64,128,128]{2,0,1:T(8,128)(2,1)}, u32[]{:S(2)}) copy-start(bf16[64,128,128]{2,0,1:T(8,128)(2,1)} %copy.40) | copy-start | bytes 6291460
  39.1 14.8 %copy-start.4 = (bf16[256,256]{1,0:T(8,128)(2,1)S(1)}, bf16[256,256]{1,0:T(8,128)(2,1)}, u32[]{:S(2)}) copy-start(bf16[256,256]{1,0:T(8,128)(2,1)} %param.11) | copy-start | bytes 393220
  49.2 19.2 %all-to-all-start.1 = ((bf16[1,128,16,128]{3,2,0,1:T(8,128)(2,1)}), bf16[1,128,16,128]{3,2,0,1:T(8,128)(2,1)S(1)}, u32[]{:S(2)}, u32[]{:S(2)}) async-start(bf16[1,128,16,128]{3,2,0,1:T(8,128)(2,1)} %copy.50), calls=%async_computation.2 | async-start | bytes 1048576 | tf_op jit(solution)/shard_map/all_to_all | solution.py:146
  53.7 15.8 %copy-start.5 = (bf16[256,128]{1,0:T(8,128)(2,1)S(1)}, bf16[256,128]{1,0:T(8,128)(2,1)}, u32[]{:S(2)}) copy-start(bf16[256,128]{1,0:T(8,128)(2,1)} %param.13) | copy-start | bytes 196612
  53.7 36.4 %all-gather.2.cloned.1.call-start = ((), (), s32[]{:S(2)}) async-start(), calls=%async_computation.4 | async-start | bytes 1572864 | tf_op jit(solution)/shard_map/all_gather | solution.py:154
Sparse Core Ops, SparseCore 0:
  12.4 12.0 reduce-scatter.1
  69.6 10.6 all-gather.1

commit v2 on v1

v2 whole, which is shorter than its diff:
```python
import functools

import jax
import jax.numpy as jnp
from jax import lax
from jax.experimental import pallas as pl
from jax.experimental.pallas import tpu as pltpu
from jax.sharding import PartitionSpec as P

BLOCK = 128
MESH = pl.DeviceIdType.MESH
MIB = 2**20

damping_strength = 10.0


def legendre_inputs(order_values, nlat):
    colatitude = jnp.pi * (jnp.arange(nlat, dtype=jnp.float32) + 0.5) / nlat
    cosines = jnp.cos(colatitude)
    sines = jnp.sin(colatitude)
    weights = jnp.pi / nlat * sines
    order_float = order_values.astype(jnp.float32)[:, None]
    indices = jnp.arange(1, nlat, dtype=jnp.float32)
    log_steps = jnp.log((2.0 * indices + 1.0) / (2.0 * indices))
    below = jnp.arange(1, nlat, dtype=jnp.int32)[None, :] <= order_values[:, None]
    picked = jnp.sum(jnp.where(below, log_steps[None, :], 0.0), axis=1)
    diagonal = jnp.exp(
        0.5 * jnp.log(0.5) + 0.5 * picked[:, None] + order_float * jnp.log(sines)[None, :]
    )
    return cosines, weights, diagonal


def damping_factors(nlat):
    degrees = jnp.arange(nlat, dtype=jnp.float32)
    scaled = degrees * (degrees + 1.0) / ((nlat - 1.0) * nlat)
    return 1.0 / (1.0 + damping_strength * scaled**2) - 1.0


def silu(value):
    half = 0.5 * value
    return half + half * jnp.tanh(half)


def dot(left, right, contract):
    return lax.dot_general(left, right, (contract, ((), ())), preferred_element_type=jnp.float32)


def kernel(
    lat_size,
    scale,
    table_ref,
    cosine_ref,
    diagonal_ref,
    weight_ref,
    damping_ref,
    lit_ref,
    w_in_ref,
    w_mid_ref,
    w_out_ref,
    state_ref,
    humidity_ref,
    out_ref,
    grid,
    humid,
    partial,
    from_sibling,
    to_wave,
    by_wave,
    degrees,
    analysis,
    synthesis,
    to_lat,
    by_lat,
    sibling_part,
    wt_in,
    wt_mid,
    wt_out,
    state_sem,
    humid_sem,
    out_sem,
    pair_send,
    pair_recv,
    wave_send,
    wave_recv,
    lat_send,
    lat_recv,
    share_send,
    share_recv,
):
    rows, levels, lons = grid.shape
    nlat = lat_size * rows
    chunk = rows * rows
    me = lax.axis_index("lat")
    sibling = 1 - lax.axis_index("lev")

    loads = [
        pltpu.make_async_copy(state_ref.at[j], grid.at[j], state_sem.at[j]) for j in range(rows)
    ]
    for load in loads:
        load.start()
    humid_load = pltpu.make_async_copy(humidity_ref, humid, humid_sem)
    humid_load.start()

    barrier = pltpu.get_barrier_semaphore()
    for step in range(1, lat_size):
        pl.semaphore_signal(
            barrier,
            inc=1,
            device_id={"lat": lax.rem(me + step, lat_size)},
            device_id_type=MESH,
        )
    pl.semaphore_signal(barrier, inc=1, device_id={"lev": sibling}, device_id_type=MESH)

    for j in range(rows):
        loads[j].wait()
        sums = dot(table_ref[...], grid[j].astype(jnp.bfloat16), ((1,), (1,))) * scale
        partial[0, pl.ds(j, nlat, stride=rows), :] = sums[:nlat]
        partial[1, pl.ds(j, nlat, stride=rows), :] = sums[nlat:]

    pl.semaphore_wait(barrier, lat_size)

    middle = lat_size // 2
    order = sorted(range(1, lat_size), key=lambda step: abs(step - middle)) + [0]

    def owner(step):
        return lax.rem(me + step, lat_size)

    def source(step):
        return lax.rem(me + lat_size - step, lat_size)

    def chunk_rows(index):
        return pl.ds(pl.multiple_of(index * chunk, chunk), chunk)

    pairs = {}
    for step in order:
        place = chunk_rows(owner(step))
        pairs[step] = pltpu.make_async_remote_copy(
            src_ref=partial.at[1, place],
            dst_ref=from_sibling.at[place],
            send_sem=pair_send.at[step],
            recv_sem=pair_recv.at[step],
            device_id={"lev": sibling},
            device_id_type=MESH,
        )
        pairs[step].start()

    waves = {}
    for step in order:
        place = chunk_rows(owner(step))
        pairs[step].wait_recv()
        whole = (partial[0, place] + from_sibling[place]).astype(jnp.bfloat16)
        if step == 0:
            by_wave[me] = whole
            continue
        to_wave[place] = whole
        waves[step] = pltpu.make_async_remote_copy(
            src_ref=to_wave.at[place],
            dst_ref=by_wave.at[me],
            send_sem=wave_send.at[step],
            recv_sem=wave_recv.at[step],
            device_id={"lat": owner(step)},
            device_id_type=MESH,
        )
        waves[step].start()

    orders = me * rows + lax.broadcasted_iota(jnp.int32, diagonal_ref.shape, 0)
    order_float = orders.astype(jnp.float32)
    order_square = order_float * order_float
    cosines = cosine_ref[...]
    wide, span, lanes = degrees.shape[0], degrees.shape[1] // rows, degrees.shape[2]

    def recurrence(base, index, pair):
        previous, earlier = pair
        degree = base + index
        degree_float = degree.astype(jnp.float32)
        square = degree_float * degree_float
        lower = degree_float - 1.0
        lower_square = lower * lower
        factor_now = jnp.sqrt((4.0 * square - 1.0) / jnp.maximum(square - order_square, 1.0))
        factor_back = jnp.sqrt(
            jnp.maximum(lower_square - order_square, 0.0)
            / jnp.maximum(4.0 * lower_square - 1.0, 1.0)
        )
        general = factor_now * (cosines * previous - factor_back * earlier)
        value = jnp.where(degree == orders, diagonal_ref[...], jnp.where(degree > orders, general, 0.0))
        place = pl.ds(pl.multiple_of(index * rows, rows), rows)
        for part in range(wide):
            degrees[part, place] = value[:, part * lanes : (part + 1) * lanes]
        return value, previous

    pair = (diagonal_ref[...] * 0.0, diagonal_ref[...] * 0.0)
    for base in range(0, nlat, span):
        pair = lax.fori_loop(0, span, functools.partial(recurrence, base), pair, unroll=4)

        @pl.loop(0, rows)
        def _(m):
            picked = jnp.concatenate(
                [degrees[part, pl.ds(m, span, stride=rows), :] for part in range(wide)], axis=1
            )
            analysis[m, base : base + span, :] = (picked * weight_ref[...]).astype(jnp.bfloat16)
            synthesis[m, :, base : base + span] = picked.T.astype(jnp.bfloat16)

    wt_in[...] = w_in_ref[...].astype(jnp.float32).T.astype(jnp.bfloat16)
    wt_mid[...] = w_mid_ref[...].astype(jnp.float32).T.astype(jnp.bfloat16)
    wt_out[...] = w_out_ref[...].astype(jnp.float32).T.astype(jnp.bfloat16)
    humid_load.wait()

    def network_row(j):
        profile = jnp.concatenate([grid[j].astype(jnp.bfloat16), humid[j]], axis=0)
        first = silu(dot(wt_in[...], profile, ((1,), (0,)))).astype(jnp.bfloat16)
        second = silu(dot(wt_mid[...], first, ((1,), (0,)))).astype(jnp.bfloat16)
        heating = dot(wt_out[...], second, ((1,), (0,))).astype(jnp.bfloat16).astype(jnp.float32)
        grid[j] = grid[j] + jnp.where(lit_ref[pl.ds(j, 1), :] > 0.5, heating, 0.0)

    early = rows // 2
    pl.loop(0, early)(network_row)

    for step in order[:-1]:
        waves[step].wait_recv()

    @pl.loop(0, rows)
    def _(m):
        place = pl.ds(pl.multiple_of(m * rows, rows), rows)
        fourier = by_wave[:, place, :].reshape(nlat, levels)
        spectral = dot(analysis[m], fourier, ((1,), (0,)))
        damped = (spectral * damping_ref[...]).astype(jnp.bfloat16)
        back = dot(synthesis[m], damped, ((1,), (0,)))
        doubled = jnp.where(me * rows + m == 0, 1.0, 2.0)
        to_lat[:, place, :] = (back * doubled).astype(jnp.bfloat16).reshape(lat_size, rows, levels)

    lats = {}
    for step in order[:-1]:
        lats[step] = pltpu.make_async_remote_copy(
            src_ref=to_lat.at[owner(step)],
            dst_ref=by_lat.at[me],
            send_sem=lat_send.at[step],
            recv_sem=lat_recv.at[step],
            device_id={"lat": owner(step)},
            device_id_type=MESH,
        )
        lats[step].start()
    by_lat[me] = to_lat[me]

    pl.loop(early, rows)(network_row)

    for step in order[:-1]:
        waves[step].wait_send()
    for step in order:
        pairs[step].wait_send()

    shares = {}
    arrival = [0] + order[:-1][::-1]
    for step in arrival:
        if step:
            lats[step].wait_recv()
        origin = source(step)
        shares[step] = pltpu.make_async_remote_copy(
            src_ref=by_lat.at[origin],
            dst_ref=sibling_part.at[origin],
            send_sem=share_send.at[step],
            recv_sem=share_recv.at[step],
            device_id={"lev": sibling},
            device_id_type=MESH,
        )
        shares[step].start()
        partial[0, chunk_rows(origin)] = by_lat[origin].astype(jnp.float32)
    for step in arrival:
        origin = source(step)
        shares[step].wait_recv()
        partial[1, chunk_rows(origin)] = sibling_part[origin].astype(jnp.float32)

    stores = [
        pltpu.make_async_copy(grid.at[j], out_ref.at[j], out_sem.at[j]) for j in range(rows)
    ]
    for j in range(rows):
        own = partial[0, pl.ds(j, nlat, stride=rows), :]
        other = partial[1, pl.ds(j, nlat, stride=rows), :]
        both = jnp.concatenate([own, other], axis=0).astype(jnp.bfloat16)
        grid[j] = grid[j] + dot(both, table_ref[...], ((0,), (0,)))
        stores[j].start()

    for step in order[:-1]:
        lats[step].wait_send()
    for step in arrival:
        shares[step].wait_send()
    for store in stores:
        store.wait()


def local(state, humidity, sun_list, sun_count, w_in, w_mid, w_out):
    rows, levels, half_lon = state.shape
    per_row = half_lon // BLOCK
    nblk = rows * per_row
    lat_size = lax.axis_size("lat")
    lev_size = lax.axis_size("lev")
    nlat = rows * lat_size
    nlon = half_lon * lev_size
    lev = lax.axis_index("lev")

    row = lax.broadcasted_iota(jnp.int32, (2 * nlat, half_lon), 0)
    longitude = lev * half_lon + lax.broadcasted_iota(jnp.int32, (2 * nlat, half_lon), 1)
    second = row >= nlat
    wavenumber = jnp.where(second, row - nlat, row)
    imaginary = second != (lev == 1)
    turned = longitude * wavenumber + jnp.where(imaginary, nlon // 4, 0)
    angle = (turned % nlon).astype(jnp.float32) * (2.0 * jnp.pi / nlon)
    table = jnp.cos(angle).astype(jnp.bfloat16)

    owned = lax.axis_index("lat") * rows + jnp.arange(rows, dtype=jnp.int32)
    cosines, weights, diagonal = legendre_inputs(owned, nlat)
    damping = jnp.broadcast_to(damping_factors(nlat)[:, None], (nlat, levels))
    positions = jnp.arange(nblk, dtype=jnp.int32)
    lit = jnp.any(
        (sun_list[0, 0][None, :] == positions[:, None]) & (positions[None, :] < sun_count[0, 0]),
        axis=1,
    )
    lit = jnp.repeat(lit.astype(jnp.float32).reshape(rows, per_row), BLOCK, axis=1)

    chunk = rows * rows
    span = min(nlat, 128)
    vmem = pl.BlockSpec(memory_space=pltpu.VMEM)
    hbm = pl.BlockSpec(memory_space=pl.ANY)
    dma = pltpu.SemaphoreType.DMA
    low = jnp.bfloat16
    return pl.pallas_call(
        functools.partial(kernel, lat_size, 1.0 / nlon),
        out_shape=jax.ShapeDtypeStruct(state.shape, jnp.float32),
        in_specs=[vmem] * 9 + [hbm] * 2,
        out_specs=hbm,
        scratch_shapes=[
            pltpu.VMEM(state.shape, jnp.float32),
            pltpu.VMEM(state.shape, low),
            pltpu.VMEM((2, nlat * rows, levels), jnp.float32),
            pltpu.VMEM((nlat * rows, levels), jnp.float32),
            pltpu.VMEM((nlat * rows, levels), low),
            pltpu.VMEM((lat_size, chunk, levels), low),
            pltpu.VMEM((nlat // span, span * rows, span), jnp.float32),
            pltpu.VMEM((rows, nlat, nlat), low),
            pltpu.VMEM((rows, nlat, nlat), low),
            pltpu.VMEM((lat_size, chunk, levels), low),
            pltpu.VMEM((lat_size, chunk, levels), low),
            pltpu.VMEM((lat_size, chunk, levels), low),
            pltpu.VMEM(w_in.shape[::-1], low),
            pltpu.VMEM(w_mid.shape[::-1], low),
            pltpu.VMEM(w_out.shape[::-1], low),
            dma((rows,)),
            dma,
            dma((rows,)),
        ]
        + [dma((lat_size,))] * 8,
        compiler_params=pltpu.CompilerParams(
            collective_id=0, has_side_effects=True, vmem_limit_bytes=58 * MIB
        ),
    )(
        table,
        jnp.broadcast_to(cosines[None, :], diagonal.shape),
        diagonal,
        jnp.broadcast_to(weights[None, :], (span, nlat)),
        damping,
        lit,
        w_in,
        w_mid,
        w_out,
        state,
        humidity,
    )


def solution(mesh):
    return jax.shard_map(
        local,
        mesh=mesh,
        in_specs=(
            P(("groups", "lat"), None, "lev"),
            P(("groups", "lat"), None, "lev"),
            P(("groups", "lat"), "lev", None),
            P(("groups", "lat"), "lev"),
            P(),
            P(),
            P(),
        ),
        out_specs=P(("groups", "lat"), None, "lev"),
        check_vma=False,
    )
```

time: 107 us -> 57.5 us (0.54)
  Pallas kernels: 1.3 us -> 43.5 us
  matrix products: 40.4 us -> 0 us
  between operations: 14.3 us -> 0.74 us
  waiting for transfers between devices: 13.4 us -> 0 us
  local copies, waits for them, and re-layouts: 17.9 us -> 7.51 us
  starting transfers between devices: 10.3 us -> 0 us
  other arithmetic: 7.77 us -> 4.83 us
    pallas_call x1, Pallas kernels: 1.3 us -> 43.5 us  [local(): pl.pallas_call(functools.partial(kernel, lat_size, 1.0 / nlon), out_shape...]
    dot_general x7 -> x0, matrix products: 40.4 us -> none  [the longest x1 14.4 us: radiation_net(): jnp.einsum('bhc,hk->bkc', hidden_one, w_mid, preferred_element_type=jnp.f...]
    all_to_all x2 -> x0, starting transfers between devices: 10.1 us -> none  [the longest x1 5.6 us: local(): lax.all_to_all(fourier, 'lat', split_axis=2, concat_axis=1, tiled=True)]
    reshape x3 -> x0, local copies, waits for them, and re-layouts: 9.52 us -> none  [the longest x1 5.49 us: local(): heating_grid = heating_grid.reshape(lat_dev, levels, half_lon)]
    all_to_all x2 -> x0, waiting for transfers between devices: 7.17 us -> none  [the longest x1 7.17 us: local(): lax.all_to_all(fourier, 'lat', split_axis=2, concat_axis=1, tiled=True)]
    reduce_scatter x1 -> x0, waiting for transfers between devices: 6.21 us -> none  [local(): lax.psum_scatter(jnp.einsum('ilx,rxm->riml', state_low, selected, preferr...]
    convert_element_type x3 -> x1, local copies, waits for them, and re-layouts: 5.89 us -> 0.08 us  [local(): lit.astype(jnp.float32).reshape(rows, per_row)]
    unnamed x12 -> x2, local copies, waits for them, and re-layouts: 0.05 us -> 5.43 us
  transfers between devices with their start and end apart: 4 -> 0, of which waited for: 2 -> 0; matrix products, arithmetic and copies ran while one was open for 43% -> 0% of each run, Pallas kernels for 1% -> 0%
where the time goes in v2:
time: 57.5 us; the launch traced here: 56.5 us
  Pallas kernels  43.5 us (76%)
  local copies, waits for them, and re-layouts  7.51 us (13%)
  other arithmetic  4.83 us (8%)
  between operations  0.74 us (1%)
    pallas_call x1, Pallas kernels, local(): pl.pallas_call(functools.partial(kernel, lat_size, 1.0 / nlon), out_shape...  43.5 us
    unnamed x2, local copies, waits for them, and re-layouts  5.43 us
    convert_element_type x1, other arithmetic, local(): table = jnp.cos(angle).astype(jnp.bfloat16)  2.99 us

profile of v2, /device:TPU:1, one launch (start us, length us, event | category | flops | bytes accessed | tf_op | source)
XLA Modules:
  0.0 56.5 jit_solution(17648569275954733408)
XLA Ops:
  0.7 0.8 %fusion.6 = pred[64]{0:T(512)(128)(4,1)S(1)} fusion(s32[64]{0:T(128)} %bitcast.9, pred[64]{0:T(512)(128)(4,1)S(1)} %iota_compare_fusion.2), kind=kLoop, calls=%fused_computation.11 | loop fusion | flops 12224 | bytes 384 | tf_op jit(solution)/shard_map/reduce_or | solution.py:313
  1.7 0.2 select_reduce_fusion
  1.9 0.7 %add_exponential_fusion.diagonal_ref = f32[16,128]{1,0:T(8,128)} fusion(f32[128]{0:T(128)S(1)} %fusion.16, f32[16]{0:T(128)S(1)} %get-tuple-element.8, f32[16]{0:T(128)S(1)} %multiply_add_fusion), kind=kLoop, calls=%fused_computation.12 | loop fusion | flops 4096 | bytes 8832 | tf_op jit(solution)/shard_map/exp | solution.py:27
  2.6 0.6 %broadcast_in_dim.30.cosine_ref = f32[16,128]{1,0:T(8,128)} broadcast(f32[128]{0:T(128)S(1)} %fusion.15), dimensions={1} | broadcast | bytes 8704 | tf_op jit(solution)/shard_map/broadcast_in_dim | solution.py:356
  3.2 0.1 reshape.64
  3.2 0.1 broadcast_in_dim.56
  3.3 0.6 %copy.10 = f32[2,8,4,128]{3,1,2,0:T(8,128)} copy(f32[2,8,4,128]{3,2,1,0:T(4,128)S(1)} %bitcast.8) | data formatting | bytes 65536
  3.9 0.7 %broadcast_in_dim.55.damping_ref = f32[128,128]{1,0:T(8,128)} broadcast(f32[128]{0:T(128)S(1)} %fusion.13), dimensions={0} | broadcast | bytes 66048 | tf_op jit(solution)/shard_map/broadcast_in_dim | solution.py:311
  4.6 0.6 %broadcast_in_dim.54.weight_ref = f32[128,128]{1,0:T(8,128)} broadcast(f32[128]{0:T(128)S(1)} %broadcast_multiply_fusion), dimensions={1} | broadcast | bytes 66048 | tf_op jit(solution)/shard_map/broadcast_in_dim | solution.py:358
  5.3 3.0 %fusion.4.table_ref = bf16[256,512]{1,0:T(8,128)(2,1)} fusion(s32[256]{0:T(256)S(1)} %get-tuple-element.5, s32[256]{0:T(256)S(1)} %get-tuple-element.6, s32[512]{0:T(512)S(1)} %iota_add_fusion, pred[256]{0:T(512)(128)(4,1)S(1)} %iota_compare_fusion.1), kind=kLoop, calls=%fused_computation.7 | loop fusion | flops 2228224 | bytes 266496 | tf_op jit(solution)/shard_map/convert_element_type | solution.py:307
  8.3 43.5 %shard_map.73 = f32[16,128,512]{2,1,0:T(8,128)} custom-call(bf16[256,512]{1,0:T(8,128)(2,1)} %fusion.4.table_ref, f32[16,128]{1,0:T(8,128)} %broadcast_in_dim.30.cosine_ref, f32[16,128]{1,0:T(8,128)} %add_exponential_fusion.diagonal_ref, f32[128,128]{1,0:T(8,128)} %broadcast_in_dim.54.weight_ref, f32[128,128]{1,0:T(8,128)} %broadcast_in_dim.55.damping_ref, ...), custom_call_target="tpu_custom_call" | custom-call | tf_op jit(solution)/shard_map/pallas_call | solution.py:325
  51.7 4.8 %copy.13 = f32[16,128,512]{2,1,0:T(8,128)} copy(f32[16,128,512]{2,1,0:T(8,128)} %shard_map.73) | data formatting | bytes 8388608
  (13 shorter events, 0.2 us)

commit v3 on v2

--- a/solution.py
+++ b/solution.py
@@ -1,4 +1,5 @@
 import functools
+import math
 
 import jax
 import jax.numpy as jnp
@@ -14,26 +15,16 @@
 damping_strength = 10.0
 
 
-def legendre_inputs(order_values, nlat):
-    colatitude = jnp.pi * (jnp.arange(nlat, dtype=jnp.float32) + 0.5) / nlat
-    cosines = jnp.cos(colatitude)
-    sines = jnp.sin(colatitude)
-    weights = jnp.pi / nlat * sines
-    order_float = order_values.astype(jnp.float32)[:, None]
-    indices = jnp.arange(1, nlat, dtype=jnp.float32)
-    log_steps = jnp.log((2.0 * indices + 1.0) / (2.0 * indices))
-    below = jnp.arange(1, nlat, dtype=jnp.int32)[None, :] <= order_values[:, None]
-    picked = jnp.sum(jnp.where(below, log_steps[None, :], 0.0), axis=1)
-    diagonal = jnp.exp(
-        0.5 * jnp.log(0.5) + 0.5 * picked[:, None] + order_float * jnp.log(sines)[None, :]
-    )
-    return cosines, weights, diagonal
-
-
-def damping_factors(nlat):
-    degrees = jnp.arange(nlat, dtype=jnp.float32)
-    scaled = degrees * (degrees + 1.0) / ((nlat - 1.0) * nlat)
-    return 1.0 / (1.0 + damping_strength * scaled**2) - 1.0
+def sine(angle):
+    square = angle * angle
+    series = 1.6059044e-10
+    for term in (-2.5052108e-8, 2.7557319e-6, -1.9841270e-4, 8.3333333e-3, -0.16666667):
+        series = series * square + term
+    return angle + angle * square * series
+
+
+def iota(shape, dimension):
+    return lax.broadcasted_iota(jnp.int32, shape, dimension)
 
 
 def silu(value):
@@ -47,25 +38,26 @@
 
 def kernel(
     lat_size,
-    scale,
-    table_ref,
-    cosine_ref,
-    diagonal_ref,
-    weight_ref,
-    damping_ref,
-    lit_ref,
+    lev_size,
+    count_ref,
+    list_ref,
     w_in_ref,
     w_mid_ref,
     w_out_ref,
     state_ref,
     humidity_ref,
     out_ref,
+    back_ref,
+    table_ref,
     grid,
     humid,
     partial,
     from_sibling,
     to_wave,
     by_wave,
+    diagonal_ref,
+    damping_ref,
+    lit_ref,
     degrees,
     analysis,
     synthesis,
@@ -111,11 +103,31 @@
         )
     pl.semaphore_signal(barrier, inc=1, device_id={"lev": sibling}, device_id_type=MESH)
 
-    for j in range(rows):
+    lev = lax.axis_index("lev")
+    nlon = lons * lev_size
+    strip = min(nlat, 128)
+    for half in range(2):
+        turn = jnp.where(lev == half, 0, nlon // 4)
+        for base in range(0, nlat, strip):
+            wavenumber = base + iota((strip, lons), 0)
+            longitude = lev * lons + iota((strip, lons), 1)
+            turned = longitude * wavenumber + turn
+            phase = turned & (nlon - 1) if nlon & (nlon - 1) == 0 else turned % nlon
+            fold = nlon // 4 - jnp.minimum(phase, nlon - phase)
+            values = sine(fold.astype(jnp.float32) * (2.0 * math.pi / nlon))
+            place = half * nlat + base
+            table_ref[place : place + strip, :] = values.astype(jnp.bfloat16)
+
+    for j in range(0, rows, 2):
         loads[j].wait()
-        sums = dot(table_ref[...], grid[j].astype(jnp.bfloat16), ((1,), (1,))) * scale
-        partial[0, pl.ds(j, nlat, stride=rows), :] = sums[:nlat]
-        partial[1, pl.ds(j, nlat, stride=rows), :] = sums[nlat:]
+        loads[j + 1].wait()
+        two = grid[j : j + 2].astype(jnp.bfloat16).reshape(2 * levels, lons)
+        sums = dot(table_ref[...], two, ((1,), (1,))) * (1.0 / nlon)
+        for part in range(2):
+            for row in range(2):
+                partial[part, pl.ds(j + row, nlat, stride=rows), :] = sums[
+                    part * nlat : (part + 1) * nlat, row * levels : (row + 1) * levels
+                ]
 
     pl.semaphore_wait(barrier, lat_size)
 
@@ -163,10 +175,31 @@
         )
         waves[step].start()
 
-    orders = me * rows + lax.broadcasted_iota(jnp.int32, diagonal_ref.shape, 0)
+    orders = me * rows + iota(diagonal_ref.shape, 0)
     order_float = orders.astype(jnp.float32)
     order_square = order_float * order_float
-    cosines = cosine_ref[...]
+    place = iota(diagonal_ref.shape, 1)
+    cosines = sine((nlat - 1 - 2 * place).astype(jnp.float32) * (0.5 * math.pi / nlat))
+    near = jnp.minimum(2 * place + 1, 2 * nlat - 1 - 2 * place).astype(jnp.float32)
+    sines = sine(near * (0.5 * math.pi / nlat))
+    weights = (sines * (math.pi / nlat))[:1]
+    index_float = jnp.maximum(place, 1).astype(jnp.float32)
+    log_steps = jnp.log((2.0 * index_float + 1.0) / (2.0 * index_float))
+    picked_steps = jnp.where((place >= 1) & (place <= orders), log_steps, 0.0)
+    cumulative = jnp.sum(picked_steps, axis=1, keepdims=True)
+    diagonal_ref[...] = jnp.exp(
+        0.5 * math.log(0.5) + 0.5 * cumulative + order_float * jnp.log(sines)
+    )
+    degree_all = iota(damping_ref.shape, 0).astype(jnp.float32)
+    scaled = degree_all * (degree_all + 1.0) / ((nlat - 1.0) * nlat)
+    damping_ref[...] = 1.0 / (1.0 + damping_strength * scaled * scaled) - 1.0
+
+    nblk = list_ref.shape[-1]
+    listed = jnp.broadcast_to(list_ref[0], (nblk, nblk)) == iota((nblk, nblk), 0)
+    sunlit = listed & (iota((nblk, nblk), 1) < count_ref[0, 0])
+    lit_column = jnp.sum(jnp.where(sunlit, 1.0, 0.0), axis=1, keepdims=True)
+    lit_ref[...] = jnp.broadcast_to(lit_column, lit_ref.shape)
+    per_row = nblk // rows
     wide, span, lanes = degrees.shape[0], degrees.shape[1] // rows, degrees.shape[2]
 
     def recurrence(base, index, pair):
@@ -197,7 +230,7 @@
             picked = jnp.concatenate(
                 [degrees[part, pl.ds(m, span, stride=rows), :] for part in range(wide)], axis=1
             )
-            analysis[m, base : base + span, :] = (picked * weight_ref[...]).astype(jnp.bfloat16)
+            analysis[m, base : base + span, :] = (picked * weights).astype(jnp.bfloat16)
             synthesis[m, :, base : base + span] = picked.T.astype(jnp.bfloat16)
 
     wt_in[...] = w_in_ref[...].astype(jnp.float32).T.astype(jnp.bfloat16)
@@ -210,15 +243,18 @@
         first = silu(dot(wt_in[...], profile, ((1,), (0,)))).astype(jnp.bfloat16)
         second = silu(dot(wt_mid[...], first, ((1,), (0,)))).astype(jnp.bfloat16)
         heating = dot(wt_out[...], second, ((1,), (0,))).astype(jnp.bfloat16).astype(jnp.float32)
-        grid[j] = grid[j] + jnp.where(lit_ref[pl.ds(j, 1), :] > 0.5, heating, 0.0)
+        lit = jnp.concatenate(
+            [lit_ref[pl.ds(j * per_row + k, 1), :] for k in range(per_row)], axis=1
+        )
+        grid[j] = grid[j] + jnp.where(lit > 0.5, heating, 0.0)
 
     early = rows // 2
-    pl.loop(0, early)(network_row)
+    pl.loop(0, early, unroll=2)(network_row)
 
     for step in order[:-1]:
         waves[step].wait_recv()
 
-    @pl.loop(0, rows)
+    @pl.loop(0, rows, unroll=4)
     def _(m):
         place = pl.ds(pl.multiple_of(m * rows, rows), rows)
         fourier = by_wave[:, place, :].reshape(nlat, levels)
@@ -241,7 +277,9 @@
         lats[step].start()
     by_lat[me] = to_lat[me]
 
-    pl.loop(early, rows)(network_row)
+    pl.loop(early, rows, unroll=2)(network_row)
+    store = pltpu.make_async_copy(grid, out_ref, out_sem)
+    store.start()
 
     for step in order[:-1]:
         waves[step].wait_send()
@@ -269,22 +307,24 @@
         shares[step].wait_recv()
         partial[1, chunk_rows(origin)] = sibling_part[origin].astype(jnp.float32)
 
-    stores = [
-        pltpu.make_async_copy(grid.at[j], out_ref.at[j], out_sem.at[j]) for j in range(rows)
-    ]
     for j in range(rows):
-        own = partial[0, pl.ds(j, nlat, stride=rows), :]
-        other = partial[1, pl.ds(j, nlat, stride=rows), :]
-        both = jnp.concatenate([own, other], axis=0).astype(jnp.bfloat16)
-        grid[j] = grid[j] + dot(both, table_ref[...], ((0,), (0,)))
-        stores[j].start()
+        for part in range(2):
+            back_ref[j, part * nlat : (part + 1) * nlat, :] = partial[
+                part, pl.ds(j, nlat, stride=rows), :
+            ].astype(jnp.bfloat16)
 
     for step in order[:-1]:
         lats[step].wait_send()
     for step in arrival:
         shares[step].wait_send()
-    for store in stores:
-        store.wait()
+    store.wait()
+
+
+def inverse_kernel(warm_ref, back_ref, table_ref, out_ref):
+    rows, levels, lons = out_ref.shape
+    both = jnp.concatenate([back_ref[row] for row in range(rows)], axis=1)
+    increment = dot(both, table_ref[...], ((0,), (0,)))
+    out_ref[...] = warm_ref[...] + increment.reshape(rows, levels, lons)
 
 
 def local(state, humidity, sun_list, sun_count, w_in, w_mid, w_out):
@@ -294,39 +334,24 @@
     lat_size = lax.axis_size("lat")
     lev_size = lax.axis_size("lev")
     nlat = rows * lat_size
-    nlon = half_lon * lev_size
-    lev = lax.axis_index("lev")
-
-    row = lax.broadcasted_iota(jnp.int32, (2 * nlat, half_lon), 0)
-    longitude = lev * half_lon + lax.broadcasted_iota(jnp.int32, (2 * nlat, half_lon), 1)
-    second = row >= nlat
-    wavenumber = jnp.where(second, row - nlat, row)
-    imaginary = second != (lev == 1)
-    turned = longitude * wavenumber + jnp.where(imaginary, nlon // 4, 0)
-    angle = (turned % nlon).astype(jnp.float32) * (2.0 * jnp.pi / nlon)
-    table = jnp.cos(angle).astype(jnp.bfloat16)
-
-    owned = lax.axis_index("lat") * rows + jnp.arange(rows, dtype=jnp.int32)
-    cosines, weights, diagonal = legendre_inputs(owned, nlat)
-    damping = jnp.broadcast_to(damping_factors(nlat)[:, None], (nlat, levels))
-    positions = jnp.arange(nblk, dtype=jnp.int32)
-    lit = jnp.any(
-        (sun_list[0, 0][None, :] == positions[:, None]) & (positions[None, :] < sun_count[0, 0]),
-        axis=1,
-    )
-    lit = jnp.repeat(lit.astype(jnp.float32).reshape(rows, per_row), BLOCK, axis=1)
-
     chunk = rows * rows
     span = min(nlat, 128)
     vmem = pl.BlockSpec(memory_space=pltpu.VMEM)
     hbm = pl.BlockSpec(memory_space=pl.ANY)
     dma = pltpu.SemaphoreType.DMA
     low = jnp.bfloat16
-    return pl.pallas_call(
-        functools.partial(kernel, lat_size, 1.0 / nlon),
-        out_shape=jax.ShapeDtypeStruct(state.shape, jnp.float32),
-        in_specs=[vmem] * 9 + [hbm] * 2,
-        out_specs=hbm,
+    smem = pl.BlockSpec(memory_space=pltpu.SMEM)
+    table_shape = (2 * nlat, half_lon)
+    back_shape = (rows, 2 * nlat, levels)
+    warm, back, table = pl.pallas_call(
+        functools.partial(kernel, lat_size, lev_size),
+        out_shape=(
+            jax.ShapeDtypeStruct(state.shape, jnp.float32),
+            jax.ShapeDtypeStruct(back_shape, low),
+            jax.ShapeDtypeStruct(table_shape, low),
+        ),
+        in_specs=[smem] + [vmem] * 4 + [hbm] * 2,
+        out_specs=(hbm, vmem, vmem),
         scratch_shapes=[
             pltpu.VMEM(state.shape, jnp.float32),
             pltpu.VMEM(state.shape, low),
@@ -334,6 +359,9 @@
             pltpu.VMEM((nlat * rows, levels), jnp.float32),
             pltpu.VMEM((nlat * rows, levels), low),
             pltpu.VMEM((lat_size, chunk, levels), low),
+            pltpu.VMEM((rows, nlat), jnp.float32),
+            pltpu.VMEM((nlat, levels), jnp.float32),
+            pltpu.VMEM((nblk, BLOCK), jnp.float32),
             pltpu.VMEM((nlat // span, span * rows, span), jnp.float32),
             pltpu.VMEM((rows, nlat, nlat), low),
             pltpu.VMEM((rows, nlat, nlat), low),
@@ -345,25 +373,26 @@
             pltpu.VMEM(w_out.shape[::-1], low),
             dma((rows,)),
             dma,
-            dma((rows,)),
+            dma,
         ]
         + [dma((lat_size,))] * 8,
         compiler_params=pltpu.CompilerParams(
-            collective_id=0, has_side_effects=True, vmem_limit_bytes=58 * MIB
+            collective_id=0, has_side_effects=True, vmem_limit_bytes=(59 if nlat > 128 else 24) * MIB
         ),
-    )(
-        table,
-        jnp.broadcast_to(cosines[None, :], diagonal.shape),
-        diagonal,
-        jnp.broadcast_to(weights[None, :], (span, nlat)),
-        damping,
-        lit,
-        w_in,
-        w_mid,
-        w_out,
-        state,
-        humidity,
-    )
+    )(sun_count, sun_list, w_in, w_mid, w_out, state, humidity)
+    tall = 2
+    return pl.pallas_call(
+        inverse_kernel,
+        grid=(rows // tall,),
+        out_shape=jax.ShapeDtypeStruct(state.shape, jnp.float32),
+        in_specs=[
+            pl.BlockSpec((tall, levels, half_lon), lambda i: (i, 0, 0)),
+            pl.BlockSpec((tall, 2 * nlat, levels), lambda i: (i, 0, 0)),
+            pl.BlockSpec(table_shape, lambda i: (0, 0)),
+        ],
+        out_specs=pl.BlockSpec((tall, levels, half_lon), lambda i: (i, 0, 0)),
+        compiler_params=pltpu.CompilerParams(vmem_limit_bytes=16 * MIB),
+    )(warm, back, table)
 
 
 def solution(mesh):

time: 57.5 us -> 48.5 us (0.84)
  other arithmetic: 4.83 us -> 0 us
  Pallas kernels: 43.5 us -> 40.3 us
    pallas_call x1 -> x2, Pallas kernels: 43.5 us -> 40.3 us  [the longest x1 35.9 us: local(): pl.pallas_call(functools.partial(kernel, lat_size, lev_size), out_shape=(...]
    convert_element_type x2 -> x0, other arithmetic: 3 us -> none  [the longest x1 2.99 us: local(): table = jnp.cos(angle).astype(jnp.bfloat16)]
    broadcast_in_dim x4 -> x0, local copies, waits for them, and re-layouts: 2.01 us -> none  [the longest x1 0.69 us: local(): damping = jnp.broadcast_to(damping_factors(nlat)[:, None], (nlat, levels))]
    unnamed x2 -> x12, local copies, waits for them, and re-layouts: 5.43 us -> 7.07 us
    reduce_or x1 -> x0, other arithmetic: 0.77 us -> none  [local(): jnp.any((sun_list[0, 0][None, :] == positions[:, None]) & (positions[None...]
    exp x1 -> x0, other arithmetic: 0.67 us -> none  [legendre_inputs(): jnp.exp(0.5 * jnp.log(0.5) + 0.5 * picked[:, None] + order_float * jnp.lo...]
where the time goes in v3:
time: 48.5 us; the launch traced here: 48.1 us
  Pallas kernels  40.3 us (83%)
  local copies, waits for them, and re-layouts  7.07 us (15%)
  between operations  0.67 us (1%)
    pallas_call x1, Pallas kernels, local(): pl.pallas_call(functools.partial(kernel, lat_size, lev_size), out_shape=(...  35.9 us
    unnamed x12, local copies, waits for them, and re-layouts  7.07 us
    pallas_call x1, Pallas kernels, local(): pl.pallas_call(inverse_kernel, grid=(rows // tall,), out_shape=jax.ShapeD...  4.47 us

profile of v3, /device:TPU:1, one launch (start us, length us, event | category | flops | bytes accessed | tf_op | source)
XLA Modules:
  0.0 48.1 jit_solution(12059236658336833192)
XLA Ops:
  0.7 0.0 copy-start
  0.7 2.2 %copy-done = f32[16,128,512]{2,1,0:T(8,128)S(1)} copy-done((f32[16,128,512]{2,1,0:T(8,128)S(1)}, f32[16,128,512]{2,1,0:T(8,128)}, u32[]{:S(2)}) %copy-start) | copy-done | bytes 4194328
  2.8 0.0 copy-start.1
  2.8 1.6 %copy-done.1 = bf16[16,128,512]{2,1,0:T(8,128)(2,1)S(1)} copy-done((bf16[16,128,512]{2,1,0:T(8,128)(2,1)S(1)}, bf16[16,128,512]{2,1,0:T(8,128)(2,1)}, u32[]{:S(2)}) %copy-start.1) | copy-done | bytes 2097176
  4.4 0.0 copy-start.2
  4.4 0.9 %copy-done.2 = bf16[256,256]{1,0:T(8,128)(2,1)S(1)} copy-done((bf16[256,256]{1,0:T(8,128)(2,1)S(1)}, bf16[256,256]{1,0:T(8,128)(2,1)}, u32[]{:S(2)}) %copy-start.2) | copy-done | bytes 131096
  5.3 0.0 copy-start.3
  5.3 0.9 %copy-done.3 = bf16[256,256]{1,0:T(8,128)(2,1)S(1)} copy-done((bf16[256,256]{1,0:T(8,128)(2,1)S(1)}, bf16[256,256]{1,0:T(8,128)(2,1)}, u32[]{:S(2)}) %copy-start.3) | copy-done | bytes 131096
  6.2 0.0 copy-start.4
  6.2 0.8 %copy-done.4 = bf16[256,128]{1,0:T(8,128)(2,1)S(1)} copy-done((bf16[256,128]{1,0:T(8,128)(2,1)S(1)}, bf16[256,128]{1,0:T(8,128)(2,1)}, u32[]{:S(2)}) %copy-start.4) | copy-done | bytes 65560
  7.1 0.0 copy-start.5
  7.1 0.7 %copy-done.5 = s32[1,1,64]{2,1,0:T(1,128)S(1)} copy-done((s32[1,1,64]{2,1,0:T(1,128)S(1)}, s32[1,1,64]{2,1,0:T(1,128)}, u32[]{:S(2)}) %copy-start.5) | copy-done | bytes 280
  7.7 35.9 %shard_map.73 = (f32[16,128,512]{2,1,0:T(8,128)S(1)}, bf16[16,256,128]{2,1,0:T(8,128)(2,1)S(1)}, bf16[256,512]{1,0:T(8,128)(2,1)S(1)}) custom-call(s32[1,1]{1,0:T(1,128)S(6)} %copy.8.count_ref, s32[1,1,64]{2,1,0:T(1,128)S(1)} %copy-done.5, bf16[256,256]{1,0:T(8,128)(2,1)S(1)} %copy-done.2, bf16[256,256]{1,0:T(8,128)(2,1)S(1)} %copy-done.3, ...), custom_call_target="tpu_custom_call" | custom-call | tf_op jit(solution)/shard_map/pallas_call | solution.py:346
  43.6 4.5 %shard_map.74 = f32[16,128,512]{2,1,0:T(8,128)} custom-call(f32[16,128,512]{2,1,0:T(8,128)S(1)} %get-tuple-element.8.warm_ref, bf16[16,256,128]{2,1,0:T(8,128)(2,1)S(1)} %get-tuple-element.9.back_ref, bf16[256,512]{1,0:T(8,128)(2,1)S(1)} %get-tuple-element.10.table_ref), custom_call_target="tpu_custom_call" | custom-call | tf_op jit(solution)/shard_map/pallas_call | solution.py:384
Async XLA Ops:
  0.7 2.2 %copy-start = (f32[16,128,512]{2,1,0:T(8,128)S(1)}, f32[16,128,512]{2,1,0:T(8,128)}, u32[]{:S(2)}) copy-start(f32[16,128,512]{2,1,0:T(8,128)} %state_ref.1) | copy-start | bytes 12582916
  2.8 1.6 %copy-start.1 = (bf16[16,128,512]{2,1,0:T(8,128)(2,1)S(1)}, bf16[16,128,512]{2,1,0:T(8,128)(2,1)}, u32[]{:S(2)}) copy-start(bf16[16,128,512]{2,1,0:T(8,128)(2,1)} %humidity_ref.1) | copy-start | bytes 6291460
  4.4 0.9 %copy-start.2 = (bf16[256,256]{1,0:T(8,128)(2,1)S(1)}, bf16[256,256]{1,0:T(8,128)(2,1)}, u32[]{:S(2)}) copy-start(bf16[256,256]{1,0:T(8,128)(2,1)} %w_in_ref.1) | copy-start | bytes 393220
  5.3 0.9 %copy-start.3 = (bf16[256,256]{1,0:T(8,128)(2,1)S(1)}, bf16[256,256]{1,0:T(8,128)(2,1)}, u32[]{:S(2)}) copy-start(bf16[256,256]{1,0:T(8,128)(2,1)} %w_mid_ref.1) | copy-start | bytes 393220
  6.2 0.8 %copy-start.4 = (bf16[256,128]{1,0:T(8,128)(2,1)S(1)}, bf16[256,128]{1,0:T(8,128)(2,1)}, u32[]{:S(2)}) copy-start(bf16[256,128]{1,0:T(8,128)(2,1)} %w_out_ref.1) | copy-start | bytes 196612
  7.1 0.7 %copy-start.5 = (s32[1,1,64]{2,1,0:T(1,128)S(1)}, s32[1,1,64]{2,1,0:T(1,128)}, u32[]{:S(2)}) copy-start(s32[1,1,64]{2,1,0:T(1,128)} %list_ref.1) | copy-start | bytes 772

commit v4 on v3

--- a/solution.py
+++ b/solution.py
@@ -52,6 +52,7 @@
     grid,
     humid,
     partial,
+    sibling_rows,
     from_sibling,
     to_wave,
     by_wave,
@@ -67,8 +68,12 @@
     wt_in,
     wt_mid,
     wt_out,
+    w_in_held,
+    w_mid_held,
+    w_out_held,
     state_sem,
     humid_sem,
+    weight_sem,
     out_sem,
     pair_send,
     pair_recv,
@@ -91,7 +96,12 @@
     for load in loads:
         load.start()
     humid_load = pltpu.make_async_copy(humidity_ref, humid, humid_sem)
-    humid_load.start()
+    weight_loads = [
+        pltpu.make_async_copy(source_ref, held, weight_sem.at[index])
+        for index, (source_ref, held) in enumerate(
+            ((w_in_ref, w_in_held), (w_mid_ref, w_mid_held), (w_out_ref, w_out_held))
+        )
+    ]
 
     barrier = pltpu.get_barrier_semaphore()
     for step in range(1, lat_size):
@@ -118,18 +128,36 @@
             place = half * nlat + base
             table_ref[place : place + strip, :] = values.astype(jnp.bfloat16)
 
+    pairs = []
     for j in range(0, rows, 2):
         loads[j].wait()
         loads[j + 1].wait()
         two = grid[j : j + 2].astype(jnp.bfloat16).reshape(2 * levels, lons)
         sums = dot(table_ref[...], two, ((1,), (1,))) * (1.0 / nlon)
-        for part in range(2):
-            for row in range(2):
-                partial[part, pl.ds(j + row, nlat, stride=rows), :] = sums[
-                    part * nlat : (part + 1) * nlat, row * levels : (row + 1) * levels
-                ]
-
-    pl.semaphore_wait(barrier, lat_size)
+        partial[1, j * nlat : (j + 1) * nlat] = sums[:nlat, :levels]
+        partial[1, (j + 1) * nlat : (j + 2) * nlat] = sums[:nlat, levels:]
+        sibling_rows[j : j + 2] = jnp.stack([sums[nlat:, :levels], sums[nlat:, levels:]])
+        if j == 0:
+            pl.semaphore_wait(barrier, lat_size)
+        pair = pltpu.make_async_remote_copy(
+            src_ref=sibling_rows.at[pl.ds(j, 2)],
+            dst_ref=from_sibling.at[pl.ds(j, 2)],
+            send_sem=pair_send.at[j // 2],
+            recv_sem=pair_recv.at[j // 2],
+            device_id={"lev": sibling},
+            device_id_type=MESH,
+        )
+        pair.start()
+        pairs.append(pair)
+
+    humid_load.start()
+    for load in weight_loads:
+        load.start()
+    for j in range(0, rows, 2):
+        pairs[j // 2].wait_recv()
+        for row in range(j, j + 2):
+            whole = partial[1, row * nlat : (row + 1) * nlat] + from_sibling[row]
+            partial[0, pl.ds(row, nlat, stride=rows), :] = whole
 
     middle = lat_size // 2
     order = sorted(range(1, lat_size), key=lambda step: abs(step - middle)) + [0]
@@ -142,25 +170,11 @@
 
     def chunk_rows(index):
         return pl.ds(pl.multiple_of(index * chunk, chunk), chunk)
-
-    pairs = {}
-    for step in order:
-        place = chunk_rows(owner(step))
-        pairs[step] = pltpu.make_async_remote_copy(
-            src_ref=partial.at[1, place],
-            dst_ref=from_sibling.at[place],
-            send_sem=pair_send.at[step],
-            recv_sem=pair_recv.at[step],
-            device_id={"lev": sibling},
-            device_id_type=MESH,
-        )
-        pairs[step].start()
 
     waves = {}
     for step in order:
         place = chunk_rows(owner(step))
-        pairs[step].wait_recv()
-        whole = (partial[0, place] + from_sibling[place]).astype(jnp.bfloat16)
+        whole = partial[0, place].astype(jnp.bfloat16)
         if step == 0:
             by_wave[me] = whole
             continue
@@ -233,9 +247,11 @@
             analysis[m, base : base + span, :] = (picked * weights).astype(jnp.bfloat16)
             synthesis[m, :, base : base + span] = picked.T.astype(jnp.bfloat16)
 
-    wt_in[...] = w_in_ref[...].astype(jnp.float32).T.astype(jnp.bfloat16)
-    wt_mid[...] = w_mid_ref[...].astype(jnp.float32).T.astype(jnp.bfloat16)
-    wt_out[...] = w_out_ref[...].astype(jnp.float32).T.astype(jnp.bfloat16)
+    for load in weight_loads:
+        load.wait()
+    wt_in[...] = w_in_held[...].astype(jnp.float32).T.astype(jnp.bfloat16)
+    wt_mid[...] = w_mid_held[...].astype(jnp.float32).T.astype(jnp.bfloat16)
+    wt_out[...] = w_out_held[...].astype(jnp.float32).T.astype(jnp.bfloat16)
     humid_load.wait()
 
     def network_row(j):
@@ -283,8 +299,8 @@
 
     for step in order[:-1]:
         waves[step].wait_send()
-    for step in order:
-        pairs[step].wait_send()
+    for pair in pairs:
+        pair.wait_send()
 
     shares = {}
     arrival = [0] + order[:-1][::-1]
@@ -350,13 +366,14 @@
             jax.ShapeDtypeStruct(back_shape, low),
             jax.ShapeDtypeStruct(table_shape, low),
         ),
-        in_specs=[smem] + [vmem] * 4 + [hbm] * 2,
+        in_specs=[smem, vmem] + [hbm] * 5,
         out_specs=(hbm, vmem, vmem),
         scratch_shapes=[
             pltpu.VMEM(state.shape, jnp.float32),
             pltpu.VMEM(state.shape, low),
             pltpu.VMEM((2, nlat * rows, levels), jnp.float32),
-            pltpu.VMEM((nlat * rows, levels), jnp.float32),
+            pltpu.VMEM((rows, nlat, levels), jnp.float32),
+            pltpu.VMEM((rows, nlat, levels), jnp.float32),
             pltpu.VMEM((nlat * rows, levels), low),
             pltpu.VMEM((lat_size, chunk, levels), low),
             pltpu.VMEM((rows, nlat), jnp.float32),
@@ -371,13 +388,18 @@
             pltpu.VMEM(w_in.shape[::-1], low),
             pltpu.VMEM(w_mid.shape[::-1], low),
             pltpu.VMEM(w_out.shape[::-1], low),
+            pltpu.VMEM(w_in.shape, low),
+            pltpu.VMEM(w_mid.shape, low),
+            pltpu.VMEM(w_out.shape, low),
             dma((rows,)),
             dma,
+            dma((3,)),
             dma,
         ]
-        + [dma((lat_size,))] * 8,
+        + [dma((rows // 2,))] * 2
+        + [dma((lat_size,))] * 6,
         compiler_params=pltpu.CompilerParams(
-            collective_id=0, has_side_effects=True, vmem_limit_bytes=(59 if nlat > 128 else 24) * MIB
+            collective_id=0, has_side_effects=True, vmem_limit_bytes=59 * MIB
         ),
     )(sun_count, sun_list, w_in, w_mid, w_out, state, humidity)
     tall = 2

time: 48.5 us -> 49.1 us (1.012)
  Pallas kernels: 40.3 us -> 43.9 us
  local copies, waits for them, and re-layouts: 7.07 us -> 4.35 us
    pallas_call x1, Pallas kernels: 35.9 us -> 39.4 us  [local(): pl.pallas_call(functools.partial(kernel, lat_size, lev_size), out_shape=(...]
    unnamed x12 -> x6, local copies, waits for them, and re-layouts: 7.07 us -> 4.35 us
where the time goes in v4:
time: 49.1 us; the launch traced here: 48.9 us
  Pallas kernels  43.9 us (89%)
  local copies, waits for them, and re-layouts  4.35 us (9%)
  between operations  0.67 us (1%)
    pallas_call x1, Pallas kernels, local(): pl.pallas_call(functools.partial(kernel, lat_size, lev_size), out_shape=(...  39.4 us
    pallas_call x1, Pallas kernels, local(): pl.pallas_call(inverse_kernel, grid=(rows // tall,), out_shape=jax.ShapeD...  4.45 us
    unnamed x6, local copies, waits for them, and re-layouts  4.35 us

profile of v4, /device:TPU:1, one launch (start us, length us, event | category | flops | bytes accessed | tf_op | source)
XLA Modules:
  0.0 48.9 jit_solution(4662662665822980380)
XLA Ops:
  0.7 39.4 %shard_map.73 = (f32[16,128,512]{2,1,0:T(8,128)}, bf16[16,256,128]{2,1,0:T(8,128)(2,1)}, bf16[256,512]{1,0:T(8,128)(2,1)}) custom-call(s32[1,1]{1,0:T(1,128)S(6)} %copy.8.count_ref, s32[1,1,64]{2,1,0:T(1,128)} %list_ref.1, bf16[256,256]{1,0:T(8,128)(2,1)} %w_in_ref.1, bf16[256,256]{1,0:T(8,128)(2,1)} %w_mid_ref.1, bf16[256,128]{1,0:T(8,128)(2,1)} %w_out_ref.1, ...), custom_call_target="tpu_custom_call" | custom-call | tf_op jit(solution)/shard_map/pallas_call | solution.py:362
  40.1 0.0 copy-start
  40.1 2.2 %copy-done = f32[16,128,512]{2,1,0:T(8,128)S(1)} copy-done((f32[16,128,512]{2,1,0:T(8,128)S(1)}, f32[16,128,512]{2,1,0:T(8,128)}, u32[]{:S(2)}) %copy-start) | copy-done | bytes 4194328
  42.3 0.0 copy-start.1
  42.3 1.2 %copy-done.1 = bf16[16,256,128]{2,1,0:T(8,128)(2,1)S(1)} copy-done((bf16[16,256,128]{2,1,0:T(8,128)(2,1)S(1)}, bf16[16,256,128]{2,1,0:T(8,128)(2,1)}, u32[]{:S(2)}) %copy-start.1) | copy-done | bytes 1048600
  43.5 0.0 copy-start.2
  43.5 0.9 %copy-done.2 = bf16[256,512]{1,0:T(8,128)(2,1)S(1)} copy-done((bf16[256,512]{1,0:T(8,128)(2,1)S(1)}, bf16[256,512]{1,0:T(8,128)(2,1)}, u32[]{:S(2)}) %copy-start.2) | copy-done | bytes 262168
  44.4 4.5 %shard_map.74 = f32[16,128,512]{2,1,0:T(8,128)} custom-call(f32[16,128,512]{2,1,0:T(8,128)S(1)} %copy-done, bf16[16,256,128]{2,1,0:T(8,128)(2,1)S(1)} %copy-done.1, bf16[256,512]{1,0:T(8,128)(2,1)S(1)} %copy-done.2), custom_call_target="tpu_custom_call" | custom-call | tf_op jit(solution)/shard_map/pallas_call | solution.py:406
Async XLA Ops:
  40.1 2.2 %copy-start = (f32[16,128,512]{2,1,0:T(8,128)S(1)}, f32[16,128,512]{2,1,0:T(8,128)}, u32[]{:S(2)}) copy-start(f32[16,128,512]{2,1,0:T(8,128)} %get-tuple-element.8.warm_ref) | copy-start | bytes 12582916
  42.3 1.2 %copy-start.1 = (bf16[16,256,128]{2,1,0:T(8,128)(2,1)S(1)}, bf16[16,256,128]{2,1,0:T(8,128)(2,1)}, u32[]{:S(2)}) copy-start(bf16[16,256,128]{2,1,0:T(8,128)(2,1)} %get-tuple-element.9.back_ref) | copy-start | bytes 3145732
  43.5 0.9 %copy-start.2 = (bf16[256,512]{1,0:T(8,128)(2,1)S(1)}, bf16[256,512]{1,0:T(8,128)(2,1)}, u32[]{:S(2)}) copy-start(bf16[256,512]{1,0:T(8,128)(2,1)} %get-tuple-element.10.table_ref) | copy-start | bytes 786436

commit v5 on v4

--- a/solution.py
+++ b/solution.py
@@ -413,7 +413,7 @@
             pl.BlockSpec(table_shape, lambda i: (0, 0)),
         ],
         out_specs=pl.BlockSpec((tall, levels, half_lon), lambda i: (i, 0, 0)),
-        compiler_params=pltpu.CompilerParams(vmem_limit_bytes=16 * MIB),
+        compiler_params=pltpu.CompilerParams(vmem_limit_bytes=59 * MIB),
     )(warm, back, table)
 
 

time: 49.1 us -> 48 us (0.978)
  local copies, waits for them, and re-layouts: 4.35 us -> 0 us
  Pallas kernels: 43.9 us -> 47.1 us
    unnamed x6 -> x0, local copies, waits for them, and re-layouts: 4.35 us -> none
    pallas_call x1, Pallas kernels: 4.45 us -> 7.63 us  [local(): pl.pallas_call(inverse_kernel, grid=(rows // tall,), out_shape=jax.ShapeD...]
where the time goes in v5:
time: 48 us; the launch traced here: 47.7 us
  Pallas kernels  47.1 us (98%)
  between operations  0.66 us (1%)
    pallas_call x1, Pallas kernels, local(): pl.pallas_call(functools.partial(kernel, lat_size, lev_size), out_shape=(...  39.4 us
    pallas_call x1, Pallas kernels, local(): pl.pallas_call(inverse_kernel, grid=(rows // tall,), out_shape=jax.ShapeD...  7.63 us

profile of v5, /device:TPU:1, one launch (start us, length us, event | category | flops | bytes accessed | tf_op | source)
XLA Modules:
  0.0 47.7 jit_solution(5377618891573548189)
XLA Ops:
  0.7 39.4 %shard_map.73 = (f32[16,128,512]{2,1,0:T(8,128)}, bf16[16,256,128]{2,1,0:T(8,128)(2,1)}, bf16[256,512]{1,0:T(8,128)(2,1)}) custom-call(s32[1,1]{1,0:T(1,128)S(6)} %copy.8.count_ref, s32[1,1,64]{2,1,0:T(1,128)} %list_ref.1, bf16[256,256]{1,0:T(8,128)(2,1)} %w_in_ref.1, bf16[256,256]{1,0:T(8,128)(2,1)} %w_mid_ref.1, bf16[256,128]{1,0:T(8,128)(2,1)} %w_out_ref.1, ...), custom_call_target="tpu_custom_call" | custom-call | tf_op jit(solution)/shard_map/pallas_call | solution.py:362
  40.1 7.6 %shard_map.74 = f32[16,128,512]{2,1,0:T(8,128)} custom-call(f32[16,128,512]{2,1,0:T(8,128)} %get-tuple-element.8.warm_ref, bf16[16,256,128]{2,1,0:T(8,128)(2,1)} %get-tuple-element.9.back_ref, bf16[256,512]{1,0:T(8,128)(2,1)} %get-tuple-element.10.table_ref), custom_call_target="tpu_custom_call" | custom-call | tf_op jit(solution)/shard_map/pallas_call | solution.py:406
